TPU v7x, 256 devices: a whole 4x4x8 slice. The times are simulated.
256 devices in a mesh: st: 32 (over y, x, core), gl: 8 (over z).
Axes of the slice: x: 4, y: 4, z: 8, core: 2. Of those that a mesh axis runs over, the one named last changes fastest.
Arguments:
- state_emb: bfloat16 [32768, 512], P(('st', 'gl')), may hold values from -3 to 3
- goal_emb: bfloat16 [32768, 512], P(('gl', 'st')), may hold values from -3 to 3
- positive: int32 [32768], P('st'), may hold values from 0 to 32767, each once
Outputs:
- grad_state: float32 [32768, 512], P(('st', 'gl'))
- grad_goal: float32 [32768, 512], P(('gl', 'st'))
- loss: float32 [], replicated
Inputs may be any that keep to these rules, and one draw needn't show every extreme that they name: Every goal is the positive of exactly one state.
All inputs are finite; a program needn't handle non-finite values.
Results may differ from a plain program's by a relative error of at most 0.0016.
Values may be sent and summed in bfloat16 or wider, within the bound.
A program may use at most 64 MiB of HBM per device.

v0:
```python
import jax
import jax.numpy as jnp
from jax import lax
from jax.sharding import PartitionSpec as P


def body(state_emb, goal_emb, positive):
    states_all = lax.all_gather(state_emb, "gl", axis=0, tiled=True)
    goals_all = lax.all_gather(goal_emb, "st", axis=0, tiled=True)
    shard_rows = state_emb.shape[0]
    row_count = states_all.shape[0]
    column_count = goals_all.shape[0]
    feature_count = states_all.shape[1]
    st_count = lax.axis_size("st")
    gl_count = lax.axis_size("gl")
    per_shard = min(shard_rows, max(1, 256 // st_count))
    block_count = shard_rows // per_shard
    block_size = st_count * per_shard
    first_column = lax.axis_index("gl") * column_count
    goal_blocks = (
        goals_all.reshape(st_count, block_count, per_shard, feature_count)
        .transpose(1, 0, 2, 3)
        .reshape(block_count, block_size, feature_count)
    )
    shard_part = jnp.arange(st_count, dtype=jnp.int32)[None, :, None] * shard_rows
    block_part = jnp.arange(block_count, dtype=jnp.int32)[:, None, None] * per_shard
    inner_part = jnp.arange(per_shard, dtype=jnp.int32)[None, None, :]
    column_ids = (shard_part + block_part + inner_part).reshape(block_count, block_size)

    def make_logits(goal_block):
        return lax.dot_general(
            states_all, goal_block, (((1,), (1,)), ((), ())), preferred_element_type=jnp.float32
        )

    def make_hits(block_columns):
        columns = first_column + block_columns
        return positive[:, None] == columns[None, :]

    def first_pass(running, item):
        row_top, row_total, local_matched = running
        goal_block, block_columns = item
        logits = make_logits(goal_block)
        picked = jnp.where(make_hits(block_columns), logits, jnp.float32(0.0))
        new_top = jnp.maximum(row_top, jnp.max(logits, axis=1))
        row_total = row_total * jnp.exp(row_top - new_top) + jnp.sum(
            jnp.exp(logits - new_top[:, None]), axis=1
        )
        column_top = jnp.max(logits, axis=0)
        column_total = jnp.sum(jnp.exp(logits - column_top[None, :]), axis=0)
        return (
            (new_top, row_total, local_matched + jnp.sum(picked, axis=1)),
            (column_top, column_total),
        )

    start = (
        jnp.full((row_count,), -jnp.inf, jnp.float32),
        jnp.zeros((row_count,), jnp.float32),
        jnp.zeros((row_count,), jnp.float32),
    )
    (row_top_own, row_total_own, local_matched), column_parts = lax.scan(
        first_pass, start, (goal_blocks, column_ids)
    )
    row_stats = (row_top_own, row_total_own)
    column_stats = tuple((piece.reshape(column_count) for piece in column_parts))
    row_top = lax.pmax(row_stats[0], "gl")
    row_total = lax.psum(row_stats[1] * jnp.exp(row_stats[0] - row_top), "gl")
    column_top = lax.pmax(column_stats[0], "st")
    column_total = lax.psum(column_stats[1] * jnp.exp(column_stats[0] - column_top), "st")
    row_lse = row_top + jnp.log(row_total)
    col_lse = column_top + jnp.log(column_total)
    partial_value = (
        jnp.sum(row_lse) / gl_count + jnp.sum(col_lse) / st_count - 2.0 * jnp.sum(local_matched)
    )
    loss = lax.psum(partial_value, ("st", "gl")) / (2.0 * row_count * st_count)

    def second_pass(state_total, item):
        goal_block, block_columns, lse_block = item
        logits = make_logits(goal_block)
        probs = 0.5 * (jnp.exp(logits - row_lse[:, None]) + jnp.exp(logits - lse_block[None, :]))
        weights = (
            probs - jnp.where(make_hits(block_columns), jnp.float32(1.0), jnp.float32(0.0))
        ).astype(jnp.bfloat16)
        state_total = state_total + jnp.dot(weights, goal_block, preferred_element_type=jnp.float32)
        goal_term = lax.dot_general(
            weights, states_all, (((0,), (0,)), ((), ())), preferred_element_type=jnp.float32
        )
        return (state_total, goal_term)

    lse_blocks = col_lse.reshape(block_count, block_size)
    state_total, goal_parts = lax.scan(
        second_pass,
        jnp.zeros((row_count, feature_count), jnp.float32),
        (goal_blocks, column_ids, lse_blocks),
    )
    goal_parts = lax.psum_scatter(goal_parts, "st", scatter_dimension=1, tiled=True)
    goal_total = goal_parts.reshape(shard_rows, feature_count)
    grad_state = lax.psum_scatter(state_total, "gl", scatter_dimension=0, tiled=True)
    return (grad_state, goal_total, loss)


def solution(mesh):
    return jax.shard_map(
        body,
        mesh=mesh,
        in_specs=(P(("st", "gl"), None), P(("gl", "st"), None), P("st")),
        out_specs=(P(("st", "gl"), None), P(("gl", "st"), None), P()),
        check_vma=False,
    )
```

profile of v0, /device:TPU:1, one launch (start us, length us, event | category | flops | bytes accessed | tf_op | source)
XLA Modules:
  0.0 651.7 jit_solution(3879219730762354090)
XLA Ops:
  9.1 56.8 %all-gather.3.cloned.1.call-done = bf16[4096,512]{1,0:T(8,128)(2,1)} async-done(((bf16[128,512]{1,0:T(8,128)(2,1)}), bf16[4096,512]{1,0:T(8,128)(2,1)}) %all-gather.3.cloned.1.call-update) | async-done | bytes 4194320 | tf_op jit(solution)/shard_map/all_gather | solution.py:9
  65.9 4.6 copy.13
  70.5 29.8 %all-gather.5.cloned.1.call-done = bf16[1024,512]{1,0:T(8,128)(2,1)} async-done(((bf16[128,512]{1,0:T(8,128)(2,1)}), bf16[1024,512]{1,0:T(8,128)(2,1)}) %all-gather.5.cloned.1.call-update) | async-done | bytes 1048592 | tf_op jit(solution)/shard_map/all_gather | solution.py:8
  100.4 39.9 %while.32 = (s32[]{:T(128)}, f32[1024]{0:T(1024)S(1)}, f32[1024]{0:T(1024)S(1)}, f32[1024]{0:T(1024)S(1)}, f32[16,256]{1,0:T(8,128)S(1)}, /*index=5*/f32[16,256]...) while((s32[]{:T(128)}, f32[1024]{0:T(1024)S(1)}, ...), condition=%wide.region_6.7_spmd.clone, body=%wide.region_0.6_spmd.clone.sunk | while | flops 270800640 | bytes 3492004 | solution.py:60
  100.4 1.9 fusion.41
  102.9 1.9 fusion.41
  105.4 1.9 fusion.41
  107.8 1.9 fusion.41
  110.3 1.9 fusion.41
  112.8 1.9 fusion.41
  115.3 1.9 fusion.41
  117.8 1.9 fusion.41
  120.3 1.9 fusion.41
  122.8 1.9 fusion.41
  125.3 1.9 fusion.41
  127.8 1.9 fusion.41
  130.3 1.9 fusion.41
  132.8 1.9 fusion.41
  135.3 1.9 fusion.41
  137.8 1.9 fusion.41
  140.3 12.1 %pmax.14 = f32[1024]{0:T(1024)S(1)} all-reduce(f32[1024]{0:T(1024)S(1)} %get-tuple-element.117), channel_id=1, replica_groups=mesh['st'=32,'gl'=8] {'gl'}, use_global_device_ids=true, to_apply=%region_9.10 | all-reduce | flops 1024 | bytes 8192 | tf_op jit(solution)/shard_map/pmax | solution.py:65
  152.3 11.1 %psum.21 = f32[1024]{0:T(1024)S(1)} all-reduce(f32[1024]{0:T(1024)S(1)} %exponential_multiply_fusion.1), channel_id=1, replica_groups=mesh['st'=32,'gl'=8] {'gl'}, use_global_device_ids=true, to_apply=%region_10.11 | all-reduce | flops 1024 | bytes 8192 | tf_op jit(solution)/shard_map/psum | solution.py:66
  164.1 131.1 %pmax.15 = f32[4096]{0:T(1024)S(1)} all-reduce(f32[4096]{0:T(1024)S(1)} %bitcast.92), channel_id=1, replica_groups=mesh['st'=32,'gl'=8] {'st'}, use_global_device_ids=true, to_apply=%region_7.8 | all-reduce | flops 4096 | bytes 32768 | tf_op jit(solution)/shard_map/pmax | solution.py:67
  295.2 123.8 %psum.22 = f32[4096]{0:T(1024)S(1)} all-reduce(f32[4096]{0:T(1024)S(1)} %exponential_multiply_fusion), channel_id=1, replica_groups=mesh['st'=32,'gl'=8] {'st'}, use_global_device_ids=true, to_apply=%region_8.9 | all-reduce | flops 4096 | bytes 32768 | tf_op jit(solution)/shard_map/psum | solution.py:68
  419.6 79.0 %while.33 = (s32[]{:T(128)}, f32[1024,512]{1,0:T(8,128)S(1)}, f32[16,256,512]{2,1,0:T(8,128)}, bf16[16,256,512]{2,1,0:T(8,128)(2,1)}, bf16[1024,512]{1,0:T(8,128...) while((s32[]{:T(128)}, f32[1024,512]{1,0:T(8,128)S(1)}, ...), condition=%wide.region_12.13_spmd.clone, body=%wide.region_11.12_spmd.clone.sunk | while | flops 808452352 | bytes 13121723 | solution.py:90
  419.7 2.0 fusion.49
  424.6 2.0 fusion.49
  426.6 1.6 select_add_fusion.5
  429.5 2.0 fusion.49
  434.5 2.1 fusion.49
  436.5 1.6 select_add_fusion.5
  439.4 2.0 fusion.49
  444.3 2.1 fusion.49
  449.3 2.0 fusion.49
  454.2 2.0 fusion.49
  459.1 2.1 fusion.49
  464.1 2.1 fusion.49
  466.1 1.6 select_add_fusion.5
  469.0 2.0 fusion.49
  471.1 1.6 select_add_fusion.5
  474.0 2.0 fusion.49
  478.9 2.1 fusion.49
  481.0 1.6 select_add_fusion.5
  483.9 2.0 fusion.49
  488.8 2.1 fusion.49
  493.7 2.0 fusion.49
  503.2 77.1 %psum.23 = f32[]{:T(128)} all-reduce(f32[]{:T(128)S(6)} %sub.53), channel_id=1, replica_groups=mesh['st'=32,'gl'=8] {'st','gl'}, use_global_device_ids=true, to_apply=%region_18.19 | all-reduce | flops 1 | bytes 8 | tf_op jit(solution)/shard_map/psum | solution.py:74
  581.0 63.1 %reduce-scatter.5.cloned.1.call-done = f32[16,8,512]{2,1,0:T(8,128)} async-done(((f32[16,256,512]{2,1,0:T(8,128)}), f32[16,8,512]{2,1,0:T(8,128)}) %reduce-scatter.5.cloned.1.call-update) | async-done | bytes 262160 | tf_op jit(solution)/shard_map/reduce_scatter | solution.py:95
  (238 shorter events, 52.5 us)
Async XLA Ops:
  7.2 58.7 %all-gather.3.cloned.1.call-start = ((), (), s32[]{:S(2)}) async-start(), calls=%async_computation.2 | async-start | bytes 4325376 | tf_op jit(solution)/shard_map/all_gather | solution.py:9
  7.9 92.5 %all-gather.5.cloned.1.call-start = ((), (), s32[]{:S(2)}) async-start(), calls=%async_computation.3 | async-start | bytes 1179648 | tf_op jit(solution)/shard_map/all_gather | solution.py:8
  8.6 572.3 %reduce-scatter.3.cloned.1.call-start = ((), (), s32[]{:S(2)}) async-start(), calls=%async_computation.4 | async-start | bytes 2359296 | tf_op jit(solution)/shard_map/reduce_scatter | solution.py:97
  65.9 34.5 %copy-start.2 = (s32[1024]{0:T(1024)S(1)}, s32[1024]{0:T(1024)}, u32[]{:S(2)}) copy-start(s32[1024]{0:T(1024)} %param.9) | copy-start | bytes 12292
  419.6 3.7 copy-start
  424.6 3.7 copy-start
  429.5 3.7 copy-start
  434.5 3.7 copy-start
  439.4 3.7 copy-start
  444.3 3.7 copy-start
  449.3 3.7 copy-start
  454.2 3.7 copy-start
  459.1 3.7 copy-start
  464.1 3.7 copy-start
  469.0 3.7 copy-start
  474.0 3.7 copy-start
  478.9 3.7 copy-start
  483.9 3.7 copy-start
  488.8 3.7 copy-start
  493.7 3.7 copy-start
  498.6 1.4 copy-start.1
  500.1 144.0 %reduce-scatter.5.cloned.1.call-start = ((), (), s32[]{:S(2)}) async-start(), calls=%async_computation.5 | async-start | bytes 8650752 | tf_op jit(solution)/shard_map/reduce_scatter | solution.py:95
Sparse Core Ops, SparseCore 0:
  10.6 55.2 all-gather.2
  67.7 32.6 all-gather.4
  500.2 37.6 reduce-scatter.2
  542.3 101.6 reduce-scatter.4
where the time goes:
time: 654 us; the launch traced here: 652 us
  blocking collectives  355 us (54%)
  waiting for transfers between devices  152 us (23%)
  matrix products  108 us (17%)
  between operations  17.6 us (3%)
  other arithmetic  9.86 us (2%)
  local copies, waits for them, and re-layouts  7.78 us (1%)
    pmax x1, blocking collectives, body(): column_top = lax.pmax(column_stats[0], 'st')  131 us
    psum x1, blocking collectives, body(): lax.psum(column_stats[1] * jnp.exp(column_stats[0] - column_top), 'st')  124 us
    psum x1, blocking collectives, body(): loss = lax.psum(partial_value, ('st', 'gl')) / (2.0 * row_count * st_count)  77.1 us
    reduce_scatter x1, waiting for transfers between devices, body(): lax.psum_scatter(goal_parts, 'st', scatter_dimension=1, tiled=True)  63.1 us
    dot_general x32, matrix products, make_logits(): lax.dot_general(states_all, goal_block, (((1,), (1,)), ((), ())), preferr...  62.7 us
    all_gather x1, waiting for transfers between devices, body(): goals_all = lax.all_gather(goal_emb, 'st', axis=0, tiled=True)  56.8 us
    all_gather x1, waiting for transfers between devices, body(): states_all = lax.all_gather(state_emb, 'gl', axis=0, tiled=True)  29.8 us
    dot_general x16, matrix products, second_pass(): jnp.dot(weights, goal_block, preferred_element_type=jnp.float32)  25.4 us
  transfers between devices with their start and end apart: 4, of which 3 were waited for; matrix products, arithmetic and copies ran while one was open for 1% of the time, Pallas kernels for 0%

commit v1 on v0

v1 whole, which is shorter than its diff:
```python
import functools

import jax
import jax.numpy as jnp
from jax import lax
from jax.experimental import pallas as pl
from jax.experimental.pallas import tpu as pltpu
from jax.sharding import PartitionSpec as P

MESH = pl.DeviceIdType.MESH
LOG2E = 1.4426950408889634
LN2 = 0.6931471805599453
X = 4
Q = X * X
B = 128
E = 512
UNIT = 272
STEP = 32700.0


def quantize(slabs, ref):
    top = slabs[0]
    top = jnp.abs(top)
    for slab in slabs[1:]:
        top = jnp.maximum(top, jnp.abs(slab))
    top = jnp.max(top, axis=0, keepdims=True)
    power = jnp.ceil(jnp.log2(jnp.maximum(top, 1e-30)))
    factor = jnp.exp2(-power) * STEP
    ref[128:144, :] = jnp.broadcast_to(power, (16, 128)).astype(jnp.int32).astype(jnp.int16)
    for slab, start in zip(slabs, (0, 64, 144, 208)):
        codes = jnp.round(slab * factor).astype(jnp.int32)
        ref[start : start + 64, :] = codes.astype(jnp.int16)


def restore(ref, halves=(0, 1)):
    power = ref[128:144, :].astype(jnp.int32).astype(jnp.float32)[0:1, :]
    factor = jnp.exp2(power) * (1.0 / STEP)
    starts = [s for h in halves for s in ((0, 64), (144, 208))[h]]
    return [ref[s : s + 64, :].astype(jnp.int32).astype(jnp.float32) * factor for s in starts]


def combine(parts):
    top = jnp.max(parts, axis=0)
    return top + jnp.log2(jnp.sum(jnp.exp2(parts - top[None]), axis=0))


def kernel(
    Z, state_ref, goal_ref, pos_ref, gs_out, gg_out, loss_out,
    S, G, PS, L, W, St, GS, GG, MR, SR, MC, SC,
    LR, zr_stat, LS, sib_stat, LC, xr_stat, LY, yr_stat, acc,
    ss, sr, zs, zr, xs1, xr1, xs2, xr2, loss_s, loss_r,
    ag_s, ag_r, ga_s, ga_r, sb_s, sb_r, st_s, st_r, rb_s, rb_r, rz_s, rz_r, rx_s, rx_r,
):
    st = lax.axis_index("st")
    z = lax.axis_index("gl")
    c = lax.rem(st, 2)
    chip = st // 2
    x = lax.rem(chip, X)
    y = chip // X
    H = Z // 2
    NB = 2 * Z

    def wrap(v, n):
        return lax.rem(v + n, n)

    def dev(xx, yy, zz, cc):
        return ((yy * X + xx) * 2 + cc, zz)

    sibling = dev(x, y, z, 1 - c)

    def near(axis, k):
        if axis == 0:
            return dev(wrap(x + k, X), y, z, c)
        if axis == 1:
            return dev(x, wrap(y + k, X), z, c)
        return dev(x, y, wrap(z + k, Z), c)

    def rcopy(src, dst, send, recv, to):
        return pltpu.make_async_remote_copy(
            src_ref=src, dst_ref=dst, send_sem=send, recv_sem=recv, device_id=to, device_id_type=MESH
        )

    others = [sibling]
    others += [near(2, k) for k in range(1, Z)]
    others += [near(a, k) for a in (0, 1) for k in range(1, X)]
    barrier = pltpu.get_barrier_semaphore()
    for to in others:
        pl.semaphore_signal(barrier, inc=1, device_id=to, device_id_type=MESH)

    own = c * Z + z
    S[own] = state_ref[...]
    G[chip] = goal_ref[...]
    PS[c] = pos_ref[...]
    pl.semaphore_wait(barrier, len(others))

    def z_copy(s, k):
        block = c * Z + wrap(z - s * (k - 1), Z)
        rows = pl.ds(0, 128) if k < H else (pl.ds(0, 64) if s > 0 else pl.ds(64, 64))
        ref = S.at[block, rows]
        i = 2 * (k - 1) + (s > 0)
        return rcopy(ref, ref, ag_s.at[i], ag_r.at[i], near(2, s))

    def sib_copy(zz):
        ref = S.at[c * Z + zz]
        return rcopy(ref, ref, sb_s.at[zz], sb_r.at[zz], sibling)

    def g_copy(part, phase, o, s, k):
        axis = part if phase == 0 else 1 - part
        back = wrap(-s * (k - 1), X)
        if axis == 0:
            q = wrap(y + o, X) * X + wrap(x + back, X)
        else:
            q = wrap(y + back, X) * X + wrap(x + o, X)
        start = 64 * part
        rows = pl.ds(start, 64) if k == 1 else pl.ds(start + (0 if s > 0 else 32), 32)
        ref = G.at[q, rows]
        i = ((part * 5 + (0 if phase == 0 else 1 + o % X)) * 2 + (k - 1)) * 2 + (s > 0)
        return rcopy(ref, ref, ga_s.at[i], ga_r.at[i], near(axis, s))

    started = []

    def start(copy):
        copy.start()
        started.append(copy)
        return copy

    signs = (1, -1)
    pos_copy = start(rcopy(PS.at[c], PS.at[c], sb_s.at[Z], sb_r.at[Z], sibling))
    zc = {(s, 1): start(z_copy(s, 1)) for s in signs}
    first = {(p, s, 1): start(g_copy(p, 0, 0, s, 1)) for p in (0, 1) for s in signs}
    second = {(p, 0, s, 1): start(g_copy(p, 1, 0, s, 1)) for p in (0, 1) for s in signs}
    sib = [start(sib_copy(z))]

    def first_forward():
        for p in (0, 1):
            for s in signs:
                first[p, s, 1].wait_recv()
                first[p, s, 2] = start(g_copy(p, 0, 0, s, 2))
        for p in (0, 1):
            for o in (1, -1):
                for s in signs:
                    second[p, o, s, 1] = start(g_copy(p, 1, o, s, 1))

    def first_last():
        for p in (0, 1):
            for s in signs:
                first[p, s, 2].wait_recv()
            for s in signs:
                second[p, 2, s, 1] = start(g_copy(p, 1, 2, s, 1))

    def second_forward(o):
        for p in (0, 1):
            for s in signs:
                second[p, o, s, 1].wait_recv()
                second[p, o, s, 2] = start(g_copy(p, 1, o, s, 2))

    def z_forward(k):
        for s in signs:
            zc[s, k - 1].wait_recv()
            zc[s, k] = start(z_copy(s, k))
        for s in signs:
            sib.append(start(sib_copy(wrap(z - s * (k - 1), Z))))

    first_forward()
    for k in range(2, H + 1):
        z_forward(k)
        if k == 2:
            second_forward(0)
            first_last()
        if k == 3:
            second_forward(1)
            second_forward(-1)
        if k == min(4, H):
            second_forward(2)
    for s in signs:
        zc[s, H].wait_recv()
    sib.append(start(sib_copy(wrap(z + H, Z))))
    for o in (0, 1, -1, 2):
        for p in (0, 1):
            for s in signs:
                second[p, o, s, 2].wait_recv()
    pos_copy.wait_recv()
    for copy in sib:
        copy.wait_recv()

    MC[...] = jnp.full(MC.shape, -3e38, jnp.float32)
    SC[...] = jnp.zeros(SC.shape, jnp.float32)

    def first_pass(r, carry):
        left = S[pl.ds(2 * r, 2)].reshape(256, E)

        def logits(k):
            right = G[4 * k : 4 * k + 4].reshape(512, E)
            out = lax.dot_general(
                left, right, (((1,), (1,)), ((), ())), preferred_element_type=jnp.float32
            ) * LOG2E
            L[pl.ds(pl.multiple_of(256 * r, 256), 256), 512 * k : 512 * k + 512] = out
            return out

        row_top = [None] * 8
        row_sum = [None] * 8

        def stats(k, block):
            pieces = [
                [block[32 * i : 32 * i + 32, 128 * j : 128 * j + 128] for j in range(4)] for i in range(8)
            ]
            new_rows = []
            old = MC[:, 512 * k : 512 * k + 512]
            old_top = [old[:, 128 * j : 128 * j + 128] for j in range(4)]
            col_top = list(old_top)
            for i in range(8):
                p = pieces[i]
                best = jnp.maximum(jnp.maximum(p[0], p[1]), jnp.maximum(p[2], p[3]))
                new_rows.append(best if row_top[i] is None else jnp.maximum(row_top[i], best))
                for j in range(4):
                    col_top[j] = jnp.maximum(col_top[j], jnp.max(p[j].reshape(4, 8, 128), axis=0))
            sums = SC[:, 512 * k : 512 * k + 512]
            col_sum = [
                sums[:, 128 * j : 128 * j + 128] * jnp.exp2(old_top[j] - col_top[j]) for j in range(4)
            ]
            for i in range(8):
                p = pieces[i]
                total = None if row_top[i] is None else row_sum[i] * jnp.exp2(row_top[i] - new_rows[i])
                for j in range(4):
                    term = jnp.exp2(p[j] - new_rows[i])
                    total = term if total is None else total + term
                    folded = p[j].reshape(4, 8, 128)
                    col_sum[j] = col_sum[j] + jnp.sum(jnp.exp2(folded - col_top[j][None]), axis=0)
                row_top[i] = new_rows[i]
                row_sum[i] = total
            for j in range(4):
                MC[:, 512 * k + 128 * j : 512 * k + 128 * j + 128] = col_top[j]
                SC[:, 512 * k + 128 * j : 512 * k + 128 * j + 128] = col_sum[j]

        blocks = [logits(0), logits(1)]
        for k in range(4):
            stats(k, blocks[k])
            if k + 2 < 4:
                blocks.append(logits(k + 2))
        for i in range(8):
            at = pl.ds(pl.multiple_of(256 * r + 32 * i, 32), 32)
            MR[at, :] = row_top[i]
            SR[at, :] = row_sum[i]
        return carry

    lax.fori_loop(0, NB // 2, first_pass, 0)

    for q in range(Q):
        m = MC[:, 128 * q : 128 * q + 128]
        top = jnp.max(m, axis=0, keepdims=True)
        total = jnp.sum(SC[:, 128 * q : 128 * q + 128] * jnp.exp2(m - top), axis=0, keepdims=True)
        LC[q : q + 1, :] = top + jnp.log2(total)

    def all_share(axis, n, src, dst, me, base):
        dst[me] = src[...]
        copies = []
        for k in range(1, n):
            i = base + k
            copies.append(start(rcopy(src, dst.at[me], st_s.at[i], st_r.at[i], near(axis, k))))
        return copies

    def arrive(copies):
        for copy in copies:
            copy.wait_recv()

    sx = all_share(0, X, LC, xr_stat, x, 0)

    def lane_combine(b, carry):
        at = pl.ds(pl.multiple_of(128 * b, 128), 128)
        m = MR[at, :].T
        top = jnp.max(m, axis=0, keepdims=True)
        total = jnp.sum(SR[at, :].T * jnp.exp2(m - top), axis=0, keepdims=True)
        LR[pl.ds(b, 1), :] = top + jnp.log2(total)
        return carry

    lax.fori_loop(0, NB, lane_combine, 0)
    sz = all_share(2, Z, LR, zr_stat, z, 16)
    arrive(sx)
    LY[...] = combine(xr_stat[...])
    sy = all_share(1, X, LY, yr_stat, y, 8)

    def transpose_states(b, carry):
        St[:, pl.ds(pl.multiple_of(128 * b, 128), 128)] = S[b].T
        return carry

    lax.fori_loop(0, NB, transpose_states, 0)

    lanes = lax.broadcasted_iota(jnp.int32, (128, 128), 1).astype(jnp.float32)
    first_goal = (z * (2 * Q * B) + c * B).astype(jnp.float32)
    arrive(sz)
    LS[...] = combine(zr_stat[...])
    ssib = start(rcopy(LS, sib_stat, st_s.at[0], st_r.at[0], sibling))

    def spread_positive(b, carry):
        row = PS[b // Z, pl.ds(lax.rem(b, Z), 1), :].astype(jnp.float32)
        at = pl.ds(pl.multiple_of(128 * b, 128), 128)
        SR[at, :] = jnp.broadcast_to(row, (128, 128)).T - lanes - first_goal
        return carry

    lax.fori_loop(0, NB, spread_positive, 0)
    arrive(sy)
    col_lse = combine(yr_stat[...])
    LC2 = col_lse + 1.0
    ssib.wait_recv()
    pair = jnp.stack([LS[...], sib_stat[...]])
    row_lse = combine(pair)
    LY2 = row_lse + 1.0
    zr_stat[0] = LY2

    def spread_rows(b, carry):
        at = pl.ds(pl.multiple_of(128 * b, 128), 128)
        row = zr_stat[0, pl.ds(b, 1), :]
        MR[at, :] = jnp.broadcast_to(row, (128, 128)).T
        return carry

    lax.fori_loop(0, NB, spread_rows, 0)
    xr_stat[0] = LC2
    zr_stat[1] = row_lse
    xr_stat[1] = col_lse
    acc[...] = jnp.zeros(acc.shape, jnp.float32)

    def second_pass(r, carry):
        rows = pl.ds(pl.multiple_of(256 * r, 256), 256)
        out = None
        hit_sum = acc[...]
        for k in range(4):
            for i in range(8):
                at = pl.ds(pl.multiple_of(256 * r + 32 * i, 32), 32)
                rl = MR[at, :]
                pb = SR[at, :]
                for j in range(4):
                    q = 4 * k + j
                    l = L[at, 128 * q : 128 * q + 128]
                    prob = jnp.exp2(l - rl) + jnp.exp2(l - xr_stat[0, q : q + 1, :])
                    hit = pb == jnp.float32(2 * B * q)
                    hit_sum = hit_sum + jnp.sum(jnp.where(hit, l, 0.0).reshape(4, 8, 128), axis=0)
                    W[at, 128 * q : 128 * q + 128] = jnp.where(hit, prob - 1.0, prob).astype(jnp.bfloat16)
            term = jnp.dot(
                W[rows, 512 * k : 512 * k + 512],
                G[4 * k : 4 * k + 4].reshape(512, E),
                preferred_element_type=jnp.float32,
            )
            out = term if out is None else out + term
        acc[...] = hit_sum
        GS[pl.ds(2 * r, 2)] = out.reshape(2, 128, E)
        return carry

    lax.fori_loop(0, NB // 2, second_pass, 0)

    def gs_slabs(b, u):
        return [GS[b, 64 * u : 64 * u + 64, 128 * i : 128 * i + 128] for i in range(4)]

    def rb_copy(zz):
        return rcopy(ss.at[zz], sr.at[zz], rb_s.at[zz], rb_r.at[zz], sibling)

    def give(zz, carry):
        for u in (0, 1):
            quantize(gs_slabs((1 - c) * Z + zz, u), ss.at[zz, u])
        rb_copy(zz).start()
        return carry

    lax.fori_loop(0, Z, give, 0)

    def goal_pass(t, carry):
        at = pl.ds(pl.multiple_of(256 * t, 256), 256)
        out = jnp.dot(St[...], W[:, at], preferred_element_type=jnp.float32)
        GG[2 * t] = out[:, :128]
        GG[2 * t + 1] = out[:, 128:]
        return carry

    lax.fori_loop(0, Q // 2, goal_pass, 0)

    def take(zz, carry):
        rb_copy(zz).wait_recv()
        for u in (0, 1):
            for i, part in enumerate(restore(sr.at[zz, u])):
                GS[c * Z + zz, 64 * u : 64 * u + 64, 128 * i : 128 * i + 128] += part
        return carry

    def rx_copy(p, phase, t, s, k):
        axis = 1 - p if phase == 0 else p
        sg = 0 if s > 0 else 1
        rows = pl.ds(0, UNIT) if k == 1 else (pl.ds(0, 144) if s > 0 else pl.ds(128, 144))
        kind = 0 if k == 2 else 1 + sg
        if phase == 0:
            src, dst = xs1.at[p, t, kind, rows], xr1.at[p, t, sg, k - 1, rows]
            i = ((p * X + t) * 2 + sg) * 2 + (k - 1)
        else:
            src, dst = xs2.at[p, kind, rows], xr2.at[p, sg, k - 1, rows]
            i = 32 + (p * 2 + sg) * 2 + (k - 1)
        return rcopy(src, dst, rx_s.at[i], rx_r.at[i], near(axis, s))

    def chip_at(p, phase, t, d):
        if phase == 0:
            return wrap(y + d, X) * X + t if p == 0 else t * X + wrap(x + d, X)
        return y * X + wrap(x + d, X) if p == 0 else wrap(y + d, X) * X + x

    def gg_slabs(q, p):
        return [GG[q, 256 * p + 64 * i : 256 * p + 64 * i + 64, :] for i in range(4)]

    def bufs(phase, p, t):
        return (xs1.at[p, t], xr1.at[p, t]) if phase == 0 else (xs2.at[p], xr2.at[p])

    def x_open(p, phase, t):
        out, _ = bufs(phase, p, t)
        quantize(gg_slabs(chip_at(p, phase, t, 2), p), out.at[0])
        for s in signs:
            rx_copy(p, phase, t, s, 2).start()

    def x_relay(p, phase, t):
        out, came = bufs(phase, p, t)
        for s in signs:
            sg = 0 if s > 0 else 1
            rx_copy(p, phase, t, s, 2).wait_recv()
            slabs = gg_slabs(chip_at(p, phase, t, s), p)
            for i, part in enumerate(restore(came.at[sg, 1], (sg,))):
                slabs[2 * sg + i] = slabs[2 * sg + i] + part
            quantize(slabs, out.at[1 + sg])
            rx_copy(p, phase, t, s, 1).start()

    def x_close(p, phase, t):
        _, came = bufs(phase, p, t)
        q = chip_at(p, phase, t, 0)
        for s in signs:
            rx_copy(p, phase, t, s, 1).wait_recv()
        for i, (a, b) in enumerate(zip(restore(came.at[0, 0]), restore(came.at[1, 0]))):
            GG[q, 256 * p + 64 * i : 256 * p + 64 * i + 64, :] += a + b

    def x_sent(p, phase, t):
        for s in signs:
            rx_copy(p, phase, t, s, 2).wait_send()
            rx_copy(p, phase, t, s, 1).wait_send()

    def over(step, phase):
        def both(t, carry):
            for p in (0, 1):
                step(p, phase, t)
            return carry

        lax.fori_loop(0, X, both, 0)

    over(x_open, 0)
    lax.fori_loop(0, Z, take, 0)

    def rz_copy(s, u, k):
        sg = 0 if s > 0 else 1
        i = (sg * 2 + u) * H + k - 1
        return rcopy(zs.at[i], zr.at[i], rz_s.at[i], rz_r.at[i], near(2, s))

    def z_step(k):
        for s in signs:
            sg = 0 if s > 0 else 1
            for u in (sg, 1 - sg):
                top = H if u == sg else H - 1
                if k > top:
                    continue
                slabs = gs_slabs(c * Z + wrap(z + s * k, Z), u)
                if k < top:
                    came = rz_copy(s, u, k + 1)
                    came.wait_recv()
                    parts = restore(zr.at[(sg * 2 + u) * H + k])
                    slabs = [a + b for a, b in zip(slabs, parts)]
                quantize(slabs, zs.at[(sg * 2 + u) * H + k - 1])
                rz_copy(s, u, k).start()

    own_rows = zr_stat[1, pl.ds(own, 1), :]
    own_cols = xr_stat[1, pl.ds(chip, 1), :]
    lead = lax.broadcasted_iota(jnp.int32, (8, 128), 0) == 0
    loss_s[0] = jnp.where(lead, own_rows + own_cols, 0.0) - 2.0 * acc[...]

    def loss_share(stage, axis, n):
        copies = []
        for k in range(1, n):
            i = 4 * stage + k if stage < 2 else 8 + k
            copies.append(start(rcopy(loss_s.at[stage], loss_r.at[i], st_s.at[32 + i], st_r.at[32 + i], near(axis, k))))
        return copies

    def loss_add(stage, copies, slots):
        arrive(copies)
        total = loss_s[stage]
        for i in slots:
            total = total + loss_r[i]
        return total

    z_step(H)
    l0 = loss_share(0, 0, X)
    over(x_relay, 0)
    for k in range(H - 1, 0, -1):
        z_step(k)
        if k == H - 1:
            over(x_close, 0)
            for p in (0, 1):
                x_open(p, 1, 0)
            loss_s[1] = loss_add(0, l0, range(1, X))
            l1 = loss_share(1, 1, X)
        if k == max(1, H - 2):
            for p in (0, 1):
                x_relay(p, 1, 0)
            loss_s[2] = loss_add(1, l1, range(5, 4 + X))
            l2 = loss_share(2, 2, Z)
    for p in (0, 1):
        x_close(p, 1, 0)
    loss_s[3] = loss_add(2, l2, range(9, 8 + Z))
    l3 = start(rcopy(loss_s.at[3], loss_r.at[0], st_s.at[32], st_r.at[32], sibling))
    gg_out[...] = GG[chip].T
    for s in signs:
        sg = 0 if s > 0 else 1
        for u in (0, 1):
            rz_copy(s, u, 1).wait_recv()
            for i, part in enumerate(restore(zr.at[(sg * 2 + u) * H])):
                GS[own, 64 * u : 64 * u + 64, 128 * i : 128 * i + 128] += part
    gs_out[...] = GS[own]
    total = loss_add(3, [l3], [0])
    loss_out[0, 0] = jnp.sum(total) * (LN2 / (4.0 * Q * Z * B))

    for copy in started:
        copy.wait_send()

    def given(zz, carry):
        rb_copy(zz).wait_send()
        return carry

    lax.fori_loop(0, Z, given, 0)
    over(x_sent, 0)
    for p in (0, 1):
        x_sent(p, 1, 0)
    for s in signs:
        sg = 0 if s > 0 else 1
        for u in (0, 1):
            for k in range(1, (H if u == sg else H - 1) + 1):
                rz_copy(s, u, k).wait_send()


def body(state_emb, goal_emb, positive):
    Z = lax.axis_size("gl")
    H = Z // 2
    NB = 2 * Z
    R, C = NB * B, Q * B
    vmem = pltpu.VMEM
    f32, bf16, i16 = jnp.float32, jnp.bfloat16, jnp.int16
    dma = pltpu.SemaphoreType.DMA
    scratch = [
        vmem((NB, B, E), bf16), vmem((Q, B, E), bf16), vmem((2, Z, B), jnp.int32),
        vmem((R, C), f32), vmem((R, C), bf16), vmem((E, R), bf16),
        vmem((NB, B, E), f32), vmem((Q, E, B), f32),
        vmem((R, B), f32), vmem((R, B), f32), vmem((8, C), f32), vmem((8, C), f32),
        vmem((NB, B), f32), vmem((Z, NB, B), f32), vmem((NB, B), f32), vmem((NB, B), f32),
        vmem((Q, B), f32), vmem((X, Q, B), f32), vmem((Q, B), f32), vmem((X, Q, B), f32),
        vmem((8, B), f32),
        vmem((Z, 2, UNIT, B), i16), vmem((Z, 2, UNIT, B), i16),
        vmem((4 * H, UNIT, B), i16), vmem((4 * H, UNIT, B), i16),
        vmem((2, X, 3, UNIT, B), i16), vmem((2, X, 2, 2, UNIT, B), i16),
        vmem((2, 3, UNIT, B), i16), vmem((2, 2, 2, UNIT, B), i16),
        vmem((4, 8, B), f32), vmem((8 + Z, 8, B), f32),
        dma((2 * H,)), dma((2 * H,)), dma((40,)), dma((40,)), dma((Z + 1,)), dma((Z + 1,)),
        dma((48,)), dma((48,)), dma((Z,)), dma((Z,)), dma((4 * H,)), dma((4 * H,)),
        dma((40,)), dma((40,)),
    ]
    whole = pl.BlockSpec(memory_space=pltpu.VMEM)
    grad_state, grad_goal, loss = pl.pallas_call(
        functools.partial(kernel, Z),
        out_shape=(
            jax.ShapeDtypeStruct((B, E), f32),
            jax.ShapeDtypeStruct((B, E), f32),
            jax.ShapeDtypeStruct((1, 1), f32),
        ),
        in_specs=[whole] * 3,
        out_specs=(whole, whole, pl.BlockSpec(memory_space=pltpu.SMEM)),
        scratch_shapes=scratch,
        compiler_params=pltpu.CompilerParams(
            collective_id=0, has_side_effects=True, vmem_limit_bytes=62 * 1024 * 1024
        ),
    )(state_emb, goal_emb, positive.reshape(Z, B))
    return grad_state, grad_goal, loss.reshape(())


def solution(mesh):
    return jax.shard_map(
        body,
        mesh=mesh,
        in_specs=(P(("st", "gl"), None), P(("gl", "st"), None), P("st")),
        out_specs=(P(("st", "gl"), None), P(("gl", "st"), None), P()),
        check_vma=False,
    )
```

time: 654 us -> 99.1 us (0.15)
  blocking collectives: 355 us -> 0 us
  waiting for transfers between devices: 152 us -> 0 us
  matrix products: 108 us -> 0 us
  Pallas kernels: 0 us -> 94.2 us
  between operations: 17.6 us -> 2.41 us
  other arithmetic: 9.86 us -> 0 us
    psum x3 -> x0, blocking collectives: 212 us -> none  [the longest x1 124 us: body(): lax.psum(column_stats[1] * jnp.exp(column_stats[0] - column_top), 'st')]
    pmax x2 -> x0, blocking collectives: 143 us -> none  [the longest x1 131 us: body(): column_top = lax.pmax(column_stats[0], 'st')]
    dot_general x64 -> x0, matrix products: 108 us -> none  [the longest x32 62.7 us: make_logits(): lax.dot_general(states_all, goal_block, (((1,), (1,)), ((), ())), preferr...]
    pallas_call x0 -> x1, Pallas kernels: none -> 94.2 us  [body(): pl.pallas_call(functools.partial(kernel, Z), out_shape=(jax.ShapeDtypeStr...]
    all_gather x2 -> x0, waiting for transfers between devices: 86.6 us -> none  [the longest x1 56.8 us: body(): goals_all = lax.all_gather(goal_emb, 'st', axis=0, tiled=True)]
    reduce_scatter x2 -> x0, waiting for transfers between devices: 63.1 us -> none  [the longest x1 63.1 us: body(): lax.psum_scatter(goal_parts, 'st', scatter_dimension=1, tiled=True)]
    reduce_sum x19 -> x0, other arithmetic: 9.1 us -> none  [the longest x16 7.19 us: first_pass(): column_total = jnp.sum(jnp.exp(logits - column_top[None, :]), axis=0)]
  transfers between devices with their start and end apart: 4 -> 0, of which waited for: 3 -> 0; matrix products, arithmetic and copies ran while one was open for 1% -> 0% of each run, Pallas kernels for 0% -> 0%
where the time goes in v1:
time: 99.1 us; the launch traced here: 99 us
  Pallas kernels  94.2 us (95%)
  local copies, waits for them, and re-layouts  2.42 us (2%)
  between operations  2.41 us (2%)
    pallas_call x1, Pallas kernels, body(): pl.pallas_call(functools.partial(kernel, Z), out_shape=(jax.ShapeDtypeStr...  94.2 us
    unnamed x4, local copies, waits for them, and re-layouts  2.42 us

profile of v1, /device:TPU:1, one launch (start us, length us, event | category | flops | bytes accessed | tf_op | source)
XLA Modules:
  0.0 99.0 jit_solution(10428802116453019913)
XLA Ops:
  0.6 94.2 %shard_map.58 = (f32[128,512]{1,0:T(8,128)}, f32[128,512]{1,0:T(8,128)}, f32[1,1]{1,0:T(1,128)}) custom-call(bf16[128,512]{1,0:T(8,128)(2,1)} %state_ref.1, bf16[128,512]{1,0:T(8,128)(2,1)} %goal_ref.1, s32[8,128]{1,0:T(8,128)} %bitcast.2), custom_call_target="tpu_custom_call" | custom-call | tf_op jit(solution)/shard_map/pallas_call | solution.py:560
  94.8 0.0 copy-start
  94.8 1.7 %copy.9 = f32[128,512]{1,0:T(8,128)} copy(f32[128,512]{1,0:T(8,128)} %get-tuple-element.12) | data formatting | bytes 524288
  96.5 0.0 copy-done
  96.5 0.7 copy.10
Async XLA Ops:
  94.8 1.7 %copy-start = (f32[128,512]{1,0:T(8,128)S(1)}, f32[128,512]{1,0:T(8,128)}, u32[]{:S(2)}) copy-start(f32[128,512]{1,0:T(8,128)} %get-tuple-element.13) | copy-start | bytes 786436

commit v2 on v0

v2 whole, which is shorter than its diff:
```python
import functools

import jax
import jax.numpy as jnp
from jax import lax
from jax.experimental import pallas as pl
from jax.experimental.pallas import tpu as pltpu
from jax.sharding import PartitionSpec as P

MESH = pl.DeviceIdType.MESH
LOG2E = 1.4426950408889634
LN2 = 0.6931471805599453
X = 4
Q = X * X
B = 128
E = 512
UNIT = 272
STEP = 32700.0


def quantize_all(items):
    tops = []
    for slabs, _ in items:
        top = jnp.abs(slabs[0])
        for slab in slabs[1:]:
            top = jnp.maximum(top, jnp.abs(slab))
        tops.append(jnp.max(top, axis=0, keepdims=True))
    powers = [jnp.ceil(jnp.log2(jnp.maximum(top, 1e-30))) for top in tops]
    factors = [jnp.exp2(-power) * STEP for power in powers]
    for (slabs, ref), power, factor in zip(items, powers, factors):
        ref[128:144, :] = jnp.broadcast_to(power, (16, 128)).astype(jnp.int32).astype(jnp.int16)
        for slab, start in zip(slabs, (0, 64, 144, 208)):
            ref[start : start + 64, :] = jnp.round(slab * factor).astype(jnp.int32).astype(jnp.int16)


def restore(ref):
    power = ref[128:144, :].astype(jnp.int32).astype(jnp.float32)[0:1, :]
    factor = jnp.exp2(power) * (1.0 / STEP)
    return [ref[s : s + 64, :].astype(jnp.int32).astype(jnp.float32) * factor for s in (0, 64, 144, 208)]


def combine(parts):
    top = jnp.max(parts, axis=0)
    return top + jnp.log2(jnp.sum(jnp.exp2(parts - top[None]), axis=0))


def kernel(
    Z, state_ref, goal_ref, pos_ref, gs_out, gg_out, loss_out,
    S, G, PS, L, W0, W1, St0, St1, GS, GR, GG, MR, SR, PB, MC, SC,
    LR, zr_stat, LS, sib_stat, LC, xr_stat, LY, yr_stat, acc,
    zs, zr, s1, r1, s2, r2, loss_s, loss_r, out_goal,
    in_sem, ag_s, ag_r, gf_s, gf_r, gg_s, gg_r, sb_s, sb_r, st_s, st_r, rb_s, rb_r, rz_s, rz_r,
    g1_s, g1_r, g2_s, g2_r,
):
    st = lax.axis_index("st")
    z = lax.axis_index("gl")
    c = lax.rem(st, 2)
    chip = st // 2
    x = lax.rem(chip, X)
    y = chip // X
    H = Z // 2
    NB = 2 * Z

    def wrap(v, n):
        return lax.rem(v + n, n)

    def dev(xx, yy, zz, cc):
        return ((yy * X + xx) * 2 + cc, zz)

    sibling = dev(x, y, z, 1 - c)

    f = x + c * (y - x)
    g = y + c * (x - y)

    def near(axis, k):
        if axis == "z":
            return dev(x, y, wrap(z + k, Z), c)
        ff, gg = (wrap(f + k, X), g) if axis == "f" else (f, wrap(g + k, X))
        return dev(ff + c * (gg - ff), gg + c * (ff - gg), z, c)

    def rcopy(src, dst, send, recv, to):
        return pltpu.make_async_remote_copy(
            src_ref=src, dst_ref=dst, send_sem=send, recv_sem=recv, device_id=to, device_id_type=MESH
        )

    others = [sibling]
    others += [near("z", k) for k in range(1, Z)]
    others += [near(a, k) for a in "fg" for k in range(1, X)]
    barrier = pltpu.get_barrier_semaphore()
    for to in others:
        pl.semaphore_signal(barrier, inc=1, device_id=to, device_id_type=MESH)

    home = X * f + g
    loads = [
        pltpu.make_async_copy(state_ref, S.at[c, z], in_sem.at[0]),
        pltpu.make_async_copy(goal_ref, G.at[home], in_sem.at[1]),
        pltpu.make_async_copy(pos_ref, PS.at[c], in_sem.at[2]),
    ]
    for copy in loads:
        copy.start()
    for copy in loads:
        copy.wait()
    pl.semaphore_wait(barrier, len(others))

    started = []

    def start(make, *args):
        make(*args).start()
        started.append((make, args))

    signs = (1, -1)

    def z_copy(s, k, half):
        rows = pl.ds(64 * half, 64)
        ref = S.at[c, wrap(z - s * (k - 1), Z), rows]
        i = (2 * (k - 1) + (s > 0)) * 2 + half
        return rcopy(ref, ref, ag_s.at[i], ag_r.at[i], near("z", s))

    def sib_copy(d):
        zz = wrap(z + d, Z)
        ref = S.at[c, zz]
        return rcopy(ref, ref, sb_s.at[zz], sb_r.at[zz], sibling)

    def pos_copy():
        return rcopy(PS.at[c], PS.at[c], sb_s.at[Z], sb_r.at[Z], sibling)

    def f_copy(k):
        ref = G.at[home]
        return rcopy(ref, ref, gf_s.at[k - 1], gf_r.at[k - 1], near("f", k))

    def g_copy(o, k):
        ref = G.at[X * wrap(f + o, X) + g]
        i = 3 * o + k - 1
        return rcopy(ref, ref, gg_s.at[i], gg_r.at[i], near("g", k))

    def z_piece(k, half, s):
        if k > 1:
            z_copy(s, k - 1, half).wait_recv()
        if k < H or half == (s < 0):
            start(z_copy, s, k, half)

    def z_forward(k):
        for late in (0, 1):
            for s in signs:
                z_piece(k, late ^ int(s < 0), s)
        for s in signs:
            start(sib_copy, -s * (k - 1))

    near_first = (1, 3, 2)
    for k in near_first:
        start(f_copy, k)
    for s in signs:
        z_piece(1, int(s < 0), s)
    start(pos_copy)
    MC[...] = jnp.full(MC.shape, -3e38, jnp.float32)
    SC[...] = jnp.zeros(SC.shape, jnp.float32)
    MR[...] = jnp.full(MR.shape, -3e38, jnp.float32)
    for s in signs:
        z_piece(1, int(s > 0), s)
    SR[...] = jnp.zeros(SR.shape, jnp.float32)
    for k in near_first:
        start(g_copy, 0, k)
    start(sib_copy, 0)
    for n, o in enumerate((3, 1, 2)):
        f_copy(near_first[n]).wait_recv()
        for k in near_first:
            start(g_copy, o, k)
        if n == 1:
            z_forward(2)

    lanes = lax.broadcasted_iota(jnp.int32, (128, 128), 1).astype(jnp.float32)
    first_goal = (z * (2 * Q * B) + c * B).astype(jnp.float32)
    pos_copy().wait_recv()

    def spread_positive(b, carry):
        row = PS[b // Z, pl.ds(lax.rem(b, Z), 1), :].astype(jnp.float32)
        at = pl.ds(pl.multiple_of(128 * b, 128), 128)
        PB[at, :] = jnp.broadcast_to(row, (128, 128)).T - lanes - first_goal
        return carry

    lax.fori_loop(0, NB, spread_positive, 0)

    def goals_in(o):
        for k in near_first:
            g_copy(o, k).wait_recv()

    def states_in(ds):
        for d in ds:
            sib_copy(d).wait_recv()

    def unit_logits(zz, ff):
        left = S[:, pl.ds(zz, 1)].reshape(256, E)
        right = G[pl.ds(X * ff, X)].reshape(512, E)
        return lax.dot_general(left, right, (((1,), (1,)), ((), ())), preferred_element_type=jnp.float32)

    def unit_stats(zz, ff, block):
        cols = pl.ds(pl.multiple_of(512 * ff, 512), 512)
        old = MC[:, cols]
        old_top = [old[:, 128 * j : 128 * j + 128] for j in range(4)]
        col_top = list(old_top)
        pieces, rows, new_rows = [], [], []
        for i in range(8):
            at = pl.ds(pl.multiple_of((i // 4 * Z + zz) * 128 + 32 * (i % 4), 32), 32)
            rows.append(at)
            part = block[32 * i : 32 * i + 32] * LOG2E
            L[at, cols] = part
            p = [part[:, 128 * j : 128 * j + 128] for j in range(4)]
            pieces.append(p)
            best = jnp.maximum(jnp.maximum(p[0], p[1]), jnp.maximum(p[2], p[3]))
            new_rows.append(jnp.maximum(MR[at, :], best))
            for j in range(4):
                col_top[j] = jnp.maximum(col_top[j], jnp.max(p[j].reshape(4, 8, 128), axis=0))
        sums = SC[:, cols]
        col_sum = [sums[:, 128 * j : 128 * j + 128] * jnp.exp2(old_top[j] - col_top[j]) for j in range(4)]
        for i in range(8):
            p = pieces[i]
            total = SR[rows[i], :] * jnp.exp2(MR[rows[i], :] - new_rows[i])
            for j in range(4):
                total = total + jnp.exp2(p[j] - new_rows[i])
                folded = p[j].reshape(4, 8, 128)
                col_sum[j] = col_sum[j] + jnp.sum(jnp.exp2(folded - col_top[j][None]), axis=0)
            MR[rows[i], :] = new_rows[i]
            SR[rows[i], :] = total
        MC[:, cols] = jnp.concatenate(col_top, axis=1)
        SC[:, cols] = jnp.concatenate(col_sum, axis=1)

    steps = (
        ((0, 0), (1, 0), (2, 0), (3, 0)),
        ((0, 3), (1, 3), (2, 3), (3, 3)),
        ((4, 0), (4, 3), (0, 1), (1, 1)),
        ((2, 1), (3, 1), (4, 1), (5, 0)),
        ((5, 3), (5, 1), (6, 0), (6, 3)),
        ((6, 1), (0, 2), (1, 2), (2, 2)),
        ((3, 2), (4, 2), (5, 2), (6, 2)),
        ((7, 0), (7, 3), (7, 1), (7, 2)),
    )

    def step(i, carry):
        @pl.when(i == 0)
        def _():
            goals_in(0)
            z_forward(3)
            states_in((0, 1, -1, 2))

        @pl.when(i == 1)
        def _():
            goals_in(3)

        @pl.when(i == 2)
        def _():
            goals_in(1)
            states_in((-2,))

        @pl.when(i == 3)
        def _():
            z_forward(4)
            states_in((3,))

        @pl.when(i == 4)
        def _():
            states_in((-3,))

        @pl.when(i == 5)
        def _():
            for s in signs:
                z_copy(s, H, int(s < 0)).wait_recv()
            start(sib_copy, H)
            goals_in(2)

        @pl.when(i == 7)
        def _():
            states_in((H,))

        places = []
        for j in range(4):
            n = sum(steps[m][j][0] << (3 * m) for m in range(8))
            o = sum(steps[m][j][1] << (2 * m) for m in range(8))
            n = lax.rem(jnp.right_shift(n, 3 * i), 8)
            o = lax.rem(jnp.right_shift(o, 2 * i), 4)
            away = (n + 1) // 2 * (2 * lax.rem(n, 2) - 1)
            places.append((wrap(z + away, Z), wrap(f + o, X)))
        blocks = [unit_logits(*places[0])]
        for j in range(4):
            if j < 3:
                blocks.append(unit_logits(*places[j + 1]))
            unit_stats(*places[j], blocks[j])
        return carry

    lax.fori_loop(0, 8, step, 0)

    for q in range(Q):
        m = MC[:, 128 * q : 128 * q + 128]
        top = jnp.max(m, axis=0, keepdims=True)
        total = jnp.sum(SC[:, 128 * q : 128 * q + 128] * jnp.exp2(m - top), axis=0, keepdims=True)
        LC[q : q + 1, :] = top + jnp.log2(total)

    def share_copy(axis, src, dst, me, base, k):
        return rcopy(src, dst.at[me], st_s.at[base + k], st_r.at[base + k], near(axis, k))

    def all_share(axis, n, src, dst, me, base):
        dst[me] = src[...]
        for k in range(1, n):
            start(share_copy, axis, src, dst, me, base, k)
        return [share_copy(axis, src, dst, me, base, k) for k in range(1, n)]

    def arrive(copies):
        for copy in copies:
            copy.wait_recv()

    sx = all_share("f", X, LC, xr_stat, f, 0)

    def lane_combine(b, carry):
        at = pl.ds(pl.multiple_of(128 * b, 128), 128)
        m = MR[at, :].T
        top = jnp.max(m, axis=0, keepdims=True)
        total = jnp.sum(SR[at, :].T * jnp.exp2(m - top), axis=0, keepdims=True)
        LR[pl.ds(b, 1), :] = top + jnp.log2(total)
        return carry

    lax.fori_loop(0, NB, lane_combine, 0)
    sz = all_share("z", Z, LR, zr_stat, z, 16)
    arrive(sx)
    LY[...] = combine(xr_stat[...])
    sy = all_share("g", X, LY, yr_stat, g, 8)

    def chunk_block(i, odd):
        pair = lax.rem(z // 2 + H // 2 + (1 + lax.rem(i, 2) if odd else 3 * lax.rem(i, 2)), H)
        late = i // 2
        return ((1 - c) * (1 - late) + c * late) * Z + 2 * pair

    def transpose_states(i, carry):
        for odd, out in ((0, St0), (1, St1)):
            b = chunk_block(i, odd)
            out[:, pl.ds(pl.multiple_of(256 * i, 256), 256)] = (
                S[b // Z, pl.ds(lax.rem(b, Z), 2)].reshape(256, E).T
            )
        return carry

    lax.fori_loop(0, 4, transpose_states, 0)

    arrive(sz)
    LS[...] = combine(zr_stat[...])
    def ls_copy():
        return rcopy(LS, sib_stat, st_s.at[0], st_r.at[0], sibling)

    start(ls_copy)
    arrive(sy)
    col_lse = combine(yr_stat[...])
    LC2 = col_lse + 1.0
    ls_copy().wait_recv()
    pair = jnp.stack([LS[...], sib_stat[...]])
    row_lse = combine(pair)
    LY2 = row_lse + 1.0
    zr_stat[0] = LY2

    xr_stat[0] = LC2
    loss_s[0] = ((row_lse + col_lse)[:8] + (row_lse + col_lse)[8:]) * (1.0 / NB)
    acc[...] = jnp.zeros(acc.shape, jnp.float32)

    def weights(b, out_ref, i):
        for n in (0, 1):
            at = pl.ds(pl.multiple_of(128 * (b + n), 128), 128)
            MR[at, :] = jnp.broadcast_to(zr_stat[0, pl.ds(b + n, 1), :], (128, 128)).T
        hit_sum = acc[...]
        marks = [(256 * (c * q + (1 - c) * (q % X * X + q // X))).astype(jnp.float32) for q in range(Q)]
        for n in range(8):
            at = pl.ds(pl.multiple_of(128 * b + 32 * n, 32), 32)
            rl = MR[at, :]
            pb = PB[at, :]
            for q in range(Q):
                l = L[at, 128 * q : 128 * q + 128]
                prob = jnp.exp2(l - rl) + jnp.exp2(l - xr_stat[0, q : q + 1, :])
                hit = pb == marks[q]
                hit_sum = hit_sum + jnp.sum(jnp.where(hit, l, 0.0).reshape(4, 8, 128), axis=0)
                out_ref[i, 32 * n : 32 * n + 32, 128 * q : 128 * q + 128] = jnp.where(
                    hit, prob - 1.0, prob
                ).astype(jnp.bfloat16)
        acc[...] = hit_sum

    def state_part(b, w_ref, i):
        out = jnp.dot(w_ref[i], G[...].reshape(Q * B, E), preferred_element_type=jnp.float32)
        GS[pl.ds(b, 2)] = out.reshape(2, 128, E)

    def rb_copy(i, odd):
        b = chunk_block(i, odd)
        pair = lax.rem(b, Z) // 2
        return rcopy(
            GS.at[pl.ds(b, 2)], GR.at[pl.ds(2 * pair, 2)], rb_s.at[2 * i + odd], rb_r.at[2 * i + odd], sibling
        )

    def rz_copy(s, u, k):
        sg = 0 if s > 0 else 1
        i = (sg * 2 + u) * H + k - 1
        return rcopy(zs.at[i], zr.at[i], rz_s.at[i], rz_r.at[i], near("z", s))

    def gs_slabs(zz, u):
        rows = pl.ds(64 * u, 64)
        return [
            GS[c * Z + zz, rows, 128 * i : 128 * i + 128] + GR[zz, rows, 128 * i : 128 * i + 128]
            for i in range(4)
        ]

    def z_step(k):
        items = [(s, u) for s in signs for u in (0, 1) if k <= (H if u == (s < 0) else H - 1)]
        ready = []
        for s, u in items:
            if k < (H if u == (s < 0) else H - 1):
                rz_copy(s, u, k + 1).wait_recv()
        for s, u in items:
            at = ((0 if s > 0 else 1) * 2 + u) * H + k
            slabs = gs_slabs(wrap(z + s * k, Z), u)
            if k < (H if u == (s < 0) else H - 1):
                slabs = [a + b for a, b in zip(slabs, restore(zr.at[at]))]
            ready.append((slabs, zs.at[at - 1]))
        quantize_all(ready)
        for s, u in items:
            rz_copy(s, u, k).start()

    weights(chunk_block(0, 0), W0, 0)

    def second_pass(i, carry):
        b0, b1 = chunk_block(i, 0), chunk_block(i, 1)
        weights(b1, W1, i)
        state_part(b0, W0, i)
        ahead = jnp.minimum(i + 1, 3)

        @pl.when(i < 2)
        def _():
            rb_copy(i, 0).start()

        @pl.when(i == 2)
        def _():
            rb_copy(0, 0).wait_recv()
            z_step(H)

        @pl.when(i < 3)
        def _():
            weights(chunk_block(ahead, 0), W0, ahead)
            state_part(b1, W1, i)

        @pl.when(i == 3)
        def _():
            state_part(b1, W1, i)

        @pl.when(i < 2)
        def _():
            rb_copy(i, 1).start()

        return carry

    lax.fori_loop(0, 4, second_pass, 0)
    for i, odd in ((0, 1), (1, 0), (1, 1)):
        rb_copy(i, odd).wait_recv()

    loss_s[0] = loss_s[0] - 2.0 * acc[...]

    def loss_copy(stage, axis, k):
        i = 4 * stage + k if stage < 2 else 8 + k
        return rcopy(loss_s.at[stage], loss_r.at[i], st_s.at[32 + i], st_r.at[32 + i], near(axis, k))

    def loss_share(stage, axis, n):
        for k in range(1, n):
            start(loss_copy, stage, axis, k)
        return [loss_copy(stage, axis, k) for k in range(1, n)]

    def loss_add(stage, copies, slots):
        arrive(copies)
        total = loss_s[stage]
        for i in slots:
            total = total + loss_r[i]
        return total

    l0 = loss_share(0, "f", X)

    def p1_copy(k, h):
        i = 2 * (k - 1) + h
        return rcopy(
            s1.at[k, pl.ds(2 * h, 2)], r1.at[k - 1, pl.ds(2 * h, 2)], g1_s.at[i], g1_r.at[i], near("f", k)
        )

    def halves(out):
        return [[out[256 * u + 64 * i : 256 * u + 64 * i + 64, :] for i in range(4)] for u in (0, 1)]

    def goal_pass(i, carry):
        k = lax.rem(jnp.right_shift(54, 2 * i), 4)
        ff = wrap(f + k, X)
        ready = []
        for h in (0, 1):
            at = pl.ds(pl.multiple_of((X * ff + 2 * h) * 128, 256), 256)
            out = jnp.dot(St0[...], W0[:, :, at].reshape(1024, 256), preferred_element_type=jnp.float32)
            out = out + jnp.dot(St1[...], W1[:, :, at].reshape(1024, 256), preferred_element_type=jnp.float32)
            for j in (0, 1):
                block = out[:, 128 * j : 128 * j + 128]
                GG[X * ff + 2 * h + j] = block
                for u, slabs in enumerate(halves(block)):
                    ready.append((slabs, s1.at[k, 2 * h + j, u]))
            quantize_all(ready[4 * h :])

            @pl.when(i < 3)
            def _():
                p1_copy(k, h).start()

        @pl.when(i == 0)
        def _():
            z_step(H - 1)

        @pl.when(i == 3)
        def _():
            z_step(H - 2)

        return carry

    lax.fori_loop(0, X, goal_pass, 0)
    loss_s[1] = loss_add(0, l0, range(1, X))
    l1 = loss_share(1, "g", X)

    def p2_copy(k):
        return rcopy(s2.at[k - 1], r2.at[k - 1], g2_s.at[k - 1], g2_r.at[k - 1], near("g", k))

    def summed(gg):
        blocks = halves(GG[X * f + gg])
        for k in (2, 1, 3):
            for u in (0, 1):
                blocks[u] = [a + b for a, b in zip(blocks[u], restore(r1.at[k - 1, gg, u]))]
        return blocks

    for k in (2, 1):
        for h in (0, 1):
            p1_copy(k, h).wait_recv()
    loss_s[2] = loss_add(1, l1, range(5, 4 + X))
    l2 = loss_share(2, "z", Z)
    z_step(1)
    for h in (0, 1):
        p1_copy(3, h).wait_recv()
    for k in (2, 1, 3):
        quantize_all([(slabs, s2.at[k - 1, u]) for u, slabs in enumerate(summed(wrap(g + k, X)))])
        p2_copy(k).start()
    mine = summed(g)
    loss_s[3] = loss_add(2, l2, range(9, 8 + Z))

    def loss_last():
        return rcopy(loss_s.at[3], loss_r.at[0], st_s.at[32], st_r.at[32], sibling)

    start(loss_last)
    for u in (0, 1):
        slabs = gs_slabs(z, u)
        for s in signs:
            rz_copy(s, u, 1).wait_recv()
            slabs = [a + b for a, b in zip(slabs, restore(zr.at[((0 if s > 0 else 1) * 2 + u) * H]))]
        for i, part in enumerate(slabs):
            GS[c * Z + z, 64 * u : 64 * u + 64, 128 * i : 128 * i + 128] = part
    gs_store = pltpu.make_async_copy(GS.at[c * Z + z], gs_out, in_sem.at[0])
    gs_store.start()
    for k in (1, 3, 2):
        p2_copy(k).wait_recv()
        for u in (0, 1):
            mine[u] = [a + b for a, b in zip(mine[u], restore(r2.at[k - 1, u]))]
    for u in (0, 1):
        for i, part in enumerate(mine[u]):
            GG[home, 256 * u + 64 * i : 256 * u + 64 * i + 64, :] = part
    out_goal[...] = GG[home].T
    gg_store = pltpu.make_async_copy(out_goal, gg_out, in_sem.at[1])
    gg_store.start()
    total = loss_add(3, [loss_last()], [0])
    loss_out[0, 0] = jnp.sum(total) * (LN2 / (4.0 * Q * Z * B))

    for make, args in started:
        make(*args).wait_send()
    for i in (0, 1):
        for odd in (0, 1):
            rb_copy(i, odd).wait_send()
    for k in range(1, X):
        for h in (0, 1):
            p1_copy(k, h).wait_send()
        p2_copy(k).wait_send()
    for s in signs:
        for u in (0, 1):
            for k in range(1, (H if u == (s < 0) else H - 1) + 1):
                rz_copy(s, u, k).wait_send()
    gs_store.wait()
    gg_store.wait()


def hand_over(gs_in, gg_in, loss_in, gs_out, gg_out, loss_out):
    gs_out[...] = gs_in[...]
    gg_out[...] = gg_in[...]
    loss_out[0, 0] = loss_in[0, 0]


def body(state_emb, goal_emb, positive):
    Z = lax.axis_size("gl")
    H = Z // 2
    NB = 2 * Z
    R, C = NB * B, Q * B
    vmem = pltpu.VMEM
    f32, bf16, i16 = jnp.float32, jnp.bfloat16, jnp.int16
    dma = pltpu.SemaphoreType.DMA
    scratch = [
        vmem((2, Z, B, E), bf16), vmem((Q, B, E), bf16), vmem((2, Z, B), jnp.int32),
        vmem((R, C), f32), vmem((4, 256, C), bf16), vmem((4, 256, C), bf16),
        vmem((E, R // 2), bf16), vmem((E, R // 2), bf16),
        vmem((NB, B, E), f32), vmem((Z, B, E), f32), vmem((Q, E, B), f32),
        vmem((R, B), f32), vmem((R, B), f32), vmem((R, B), f32), vmem((8, C), f32), vmem((8, C), f32),
        vmem((NB, B), f32), vmem((Z, NB, B), f32), vmem((NB, B), f32), vmem((NB, B), f32),
        vmem((Q, B), f32), vmem((X, Q, B), f32), vmem((Q, B), f32), vmem((X, Q, B), f32),
        vmem((8, B), f32),
        vmem((4 * H, UNIT, B), i16), vmem((4 * H, UNIT, B), i16),
        vmem((X, X, 2, UNIT, B), i16), vmem((X - 1, X, 2, UNIT, B), i16),
        vmem((X - 1, 2, UNIT, B), i16), vmem((X - 1, 2, UNIT, B), i16),
        vmem((4, 8, B), f32), vmem((8 + Z, 8, B), f32), vmem((B, E), f32),
        dma((3,)), dma((4 * H,)), dma((4 * H,)), dma((3,)), dma((3,)), dma((12,)), dma((12,)),
        dma((Z + 1,)), dma((Z + 1,)), dma((48,)), dma((48,)), dma((4,)), dma((4,)),
        dma((4 * H,)), dma((4 * H,)), dma((6,)), dma((6,)), dma((3,)), dma((3,)),
    ]
    there = pl.BlockSpec(memory_space=pl.ANY)
    whole = pl.BlockSpec(memory_space=pltpu.VMEM)
    scalar = pl.BlockSpec(memory_space=pltpu.SMEM)
    shapes = (
        jax.ShapeDtypeStruct((B, E), f32),
        jax.ShapeDtypeStruct((B, E), f32),
        jax.ShapeDtypeStruct((1, 1), f32),
    )
    results = pl.pallas_call(
        functools.partial(kernel, Z),
        out_shape=shapes,
        in_specs=[there] * 3,
        out_specs=(there, there, scalar),
        scratch_shapes=scratch,
        compiler_params=pltpu.CompilerParams(
            collective_id=0, has_side_effects=True, vmem_limit_bytes=62 * 1024 * 1024
        ),
    )(state_emb, goal_emb, positive.reshape(Z, B))
    grad_state, grad_goal, loss = pl.pallas_call(
        hand_over,
        out_shape=shapes,
        in_specs=[whole, whole, scalar],
        out_specs=(whole, whole, scalar),
    )(*results)
    return grad_state, grad_goal, loss.reshape(())


def solution(mesh):
    return jax.shard_map(
        body,
        mesh=mesh,
        in_specs=(P(("st", "gl"), None), P(("gl", "st"), None), P("st")),
        out_specs=(P(("st", "gl"), None), P(("gl", "st"), None), P()),
        check_vma=False,
    )
```

time: 654 us -> 85.6 us (0.13)
  blocking collectives: 355 us -> 0 us
  waiting for transfers between devices: 152 us -> 0 us
  matrix products: 108 us -> 0 us
  Pallas kernels: 0 us -> 84.8 us
  between operations: 17.6 us -> 0.64 us
  other arithmetic: 9.86 us -> 0 us
  local copies, waits for them, and re-layouts: 7.78 us -> 0 us
    psum x3 -> x0, blocking collectives: 212 us -> none  [the longest x1 124 us: body(): lax.psum(column_stats[1] * jnp.exp(column_stats[0] - column_top), 'st')]
    pmax x2 -> x0, blocking collectives: 143 us -> none  [the longest x1 131 us: body(): column_top = lax.pmax(column_stats[0], 'st')]
    dot_general x64 -> x0, matrix products: 108 us -> none  [the longest x32 62.7 us: make_logits(): lax.dot_general(states_all, goal_block, (((1,), (1,)), ((), ())), preferr...]
    all_gather x2 -> x0, waiting for transfers between devices: 86.6 us -> none  [the longest x1 56.8 us: body(): goals_all = lax.all_gather(goal_emb, 'st', axis=0, tiled=True)]
    pallas_call x0 -> x2, Pallas kernels: none -> 84.8 us  [the longest x1 82.3 us: body(): pl.pallas_call(functools.partial(kernel, Z), out_shape=shapes, in_specs=[...]
    reduce_scatter x2 -> x0, waiting for transfers between devices: 63.1 us -> none  [the longest x1 63.1 us: body(): lax.psum_scatter(goal_parts, 'st', scatter_dimension=1, tiled=True)]
    reduce_sum x19 -> x0, other arithmetic: 9.1 us -> none  [the longest x16 7.19 us: first_pass(): column_total = jnp.sum(jnp.exp(logits - column_top[None, :]), axis=0)]
  transfers between devices with their start and end apart: 4 -> 0, of which waited for: 3 -> 0; matrix products, arithmetic and copies ran while one was open for 1% -> 0% of each run, Pallas kernels for 0% -> 0%
where the time goes in v2:
time: 85.6 us; the launch traced here: 85.5 us
  Pallas kernels  84.8 us (99%)
    pallas_call x1, Pallas kernels, body(): pl.pallas_call(functools.partial(kernel, Z), out_shape=shapes, in_specs=[...  82.3 us
    pallas_call x1, Pallas kernels, body(): pl.pallas_call(hand_over, out_shape=shapes, in_specs=[whole, whole, scala...  2.48 us

profile of v2, /device:TPU:1, one launch (start us, length us, event | category | flops | bytes accessed | tf_op | source)
XLA Modules:
  0.0 85.5 jit_solution(13045894734701321816)
XLA Ops:
  0.6 82.3 %shard_map.58 = (f32[128,512]{1,0:T(8,128)}, f32[128,512]{1,0:T(8,128)}, f32[1,1]{1,0:T(1,128)}) custom-call(bf16[128,512]{1,0:T(8,128)(2,1)} %state_ref.1, bf16[128,512]{1,0:T(8,128)(2,1)} %goal_ref.1, s32[8,128]{1,0:T(8,128)} %bitcast.2), custom_call_target="tpu_custom_call" | custom-call | tf_op jit(solution)/shard_map/pallas_call | solution.py:623
  83.0 2.5 %shard_map.59 = (f32[128,512]{1,0:T(8,128)}, f32[128,512]{1,0:T(8,128)}, f32[1,1]{1,0:T(1,128)}) custom-call(f32[128,512]{1,0:T(8,128)} %get-tuple-element.9.gs_in, f32[128,512]{1,0:T(8,128)} %get-tuple-element.10.gg_in, f32[1,1]{1,0:T(1,128)} %get-tuple-element.11.loss_in), custom_call_target="tpu_custom_call" | custom-call | tf_op jit(solution)/shard_map/pallas_call | solution.py:633

commit v3 on v2

--- a/solution.py
+++ b/solution.py
@@ -46,7 +46,7 @@
 
 def kernel(
     Z, state_ref, goal_ref, pos_ref, gs_out, gg_out, loss_out,
-    S, G, PS, L, W0, W1, St0, St1, GS, GR, GG, MR, SR, PB, MC, SC,
+    S, G, PS, L, W0, W1, St, GS, GR, GG, MR, SR, PB, MC, SC,
     LR, zr_stat, LS, sib_stat, LC, xr_stat, LY, yr_stat, acc,
     zs, zr, s1, r1, s2, r2, loss_s, loss_r, out_goal,
     in_sem, ag_s, ag_r, gf_s, gf_r, gg_s, gg_r, sb_s, sb_r, st_s, st_r, rb_s, rb_r, rz_s, rz_r,
@@ -161,12 +161,16 @@
     for k in near_first:
         start(g_copy, 0, k)
     start(sib_copy, 0)
-    for n, o in enumerate((3, 1, 2)):
-        f_copy(near_first[n]).wait_recv()
+    z_forward(2)
+
+    def goals_out(o):
         for k in near_first:
             start(g_copy, o, k)
-        if n == 1:
-            z_forward(2)
+
+    f_copy(1).wait_recv()
+    goals_out(3)
+    for k in (3, 2):
+        f_copy(k).wait_recv()
 
     lanes = lax.broadcasted_iota(jnp.int32, (128, 128), 1).astype(jnp.float32)
     first_goal = (z * (2 * Q * B) + c * B).astype(jnp.float32)
@@ -198,14 +202,13 @@
         old = MC[:, cols]
         old_top = [old[:, 128 * j : 128 * j + 128] for j in range(4)]
         col_top = list(old_top)
-        pieces, rows, new_rows = [], [], []
+        rows, new_rows = [], []
         for i in range(8):
             at = pl.ds(pl.multiple_of((i // 4 * Z + zz) * 128 + 32 * (i % 4), 32), 32)
             rows.append(at)
             part = block[32 * i : 32 * i + 32] * LOG2E
             L[at, cols] = part
             p = [part[:, 128 * j : 128 * j + 128] for j in range(4)]
-            pieces.append(p)
             best = jnp.maximum(jnp.maximum(p[0], p[1]), jnp.maximum(p[2], p[3]))
             new_rows.append(jnp.maximum(MR[at, :], best))
             for j in range(4):
@@ -213,7 +216,8 @@
         sums = SC[:, cols]
         col_sum = [sums[:, 128 * j : 128 * j + 128] * jnp.exp2(old_top[j] - col_top[j]) for j in range(4)]
         for i in range(8):
-            p = pieces[i]
+            part = L[rows[i], cols]
+            p = [part[:, 128 * j : 128 * j + 128] for j in range(4)]
             total = SR[rows[i], :] * jnp.exp2(MR[rows[i], :] - new_rows[i])
             for j in range(4):
                 total = total + jnp.exp2(p[j] - new_rows[i])
@@ -226,51 +230,50 @@
 
     steps = (
         ((0, 0), (1, 0), (2, 0), (3, 0)),
-        ((0, 3), (1, 3), (2, 3), (3, 3)),
-        ((4, 0), (4, 3), (0, 1), (1, 1)),
-        ((2, 1), (3, 1), (4, 1), (5, 0)),
-        ((5, 3), (5, 1), (6, 0), (6, 3)),
+        ((4, 0), (5, 0), (6, 0), (0, 3)),
+        ((1, 3), (2, 3), (3, 3), (4, 3)),
+        ((5, 3), (6, 3), (0, 1), (1, 1)),
+        ((2, 1), (3, 1), (4, 1), (5, 1)),
         ((6, 1), (0, 2), (1, 2), (2, 2)),
         ((3, 2), (4, 2), (5, 2), (6, 2)),
         ((7, 0), (7, 3), (7, 1), (7, 2)),
     )
 
-    def step(i, carry):
+    def arrivals(i):
         @pl.when(i == 0)
         def _():
             goals_in(0)
             z_forward(3)
+            goals_out(1)
             states_in((0, 1, -1, 2))
 
         @pl.when(i == 1)
         def _():
+            goals_out(2)
+            z_forward(4)
+            states_in((-2, 3, -3))
             goals_in(3)
 
-        @pl.when(i == 2)
+        @pl.when(i == 3)
         def _():
             goals_in(1)
-            states_in((-2,))
-
-        @pl.when(i == 3)
-        def _():
-            z_forward(4)
-            states_in((3,))
 
         @pl.when(i == 4)
-        def _():
-            states_in((-3,))
-
-        @pl.when(i == 5)
         def _():
             for s in signs:
                 z_copy(s, H, int(s < 0)).wait_recv()
             start(sib_copy, H)
+
+        @pl.when(i == 5)
+        def _():
             goals_in(2)
 
         @pl.when(i == 7)
         def _():
             states_in((H,))
 
+    def step(i, carry):
+        arrivals(i)
         places = []
         for j in range(4):
             n = sum(steps[m][j][0] << (3 * m) for m in range(8))
@@ -323,20 +326,11 @@
     LY[...] = combine(xr_stat[...])
     sy = all_share("g", X, LY, yr_stat, g, 8)
 
-    def chunk_block(i, odd):
-        pair = lax.rem(z // 2 + H // 2 + (1 + lax.rem(i, 2) if odd else 3 * lax.rem(i, 2)), H)
-        late = i // 2
-        return ((1 - c) * (1 - late) + c * late) * Z + 2 * pair
-
-    def transpose_states(i, carry):
-        for odd, out in ((0, St0), (1, St1)):
-            b = chunk_block(i, odd)
-            out[:, pl.ds(pl.multiple_of(256 * i, 256), 256)] = (
-                S[b // Z, pl.ds(lax.rem(b, Z), 2)].reshape(256, E).T
-            )
-        return carry
-
-    lax.fori_loop(0, 4, transpose_states, 0)
+    def transpose_states(b, carry):
+        St[:, pl.ds(pl.multiple_of(128 * b, 128), 128)] = S[b // Z, lax.rem(b, Z)].T
+        return carry
+
+    lax.fori_loop(0, NB, transpose_states, 0)
 
     arrive(sz)
     LS[...] = combine(zr_stat[...])
@@ -357,36 +351,78 @@
     loss_s[0] = ((row_lse + col_lse)[:8] + (row_lse + col_lse)[8:]) * (1.0 / NB)
     acc[...] = jnp.zeros(acc.shape, jnp.float32)
 
-    def weights(b, out_ref, i):
-        for n in (0, 1):
-            at = pl.ds(pl.multiple_of(128 * (b + n), 128), 128)
-            MR[at, :] = jnp.broadcast_to(zr_stat[0, pl.ds(b + n, 1), :], (128, 128)).T
+    def weights(ff, b, out_ref, n):
         hit_sum = acc[...]
-        marks = [(256 * (c * q + (1 - c) * (q % X * X + q // X))).astype(jnp.float32) for q in range(Q)]
-        for n in range(8):
-            at = pl.ds(pl.multiple_of(128 * b + 32 * n, 32), 32)
+        marks = []
+        tops = []
+        for j in range(X):
+            q = X * ff + j
+            marks.append((256 * (c * q + (1 - c) * (X * j + ff))).astype(jnp.float32))
+            tops.append(xr_stat[0, pl.ds(q, 1), :])
+        for i in range(8):
+            at = pl.ds(pl.multiple_of(128 * b + 32 * i, 32), 32)
             rl = MR[at, :]
             pb = PB[at, :]
-            for q in range(Q):
-                l = L[at, 128 * q : 128 * q + 128]
-                prob = jnp.exp2(l - rl) + jnp.exp2(l - xr_stat[0, q : q + 1, :])
-                hit = pb == marks[q]
+            for j in range(X):
+                l = L[at, pl.ds(pl.multiple_of(512 * ff + 128 * j, 128), 128)]
+                prob = jnp.exp2(l - rl) + jnp.exp2(l - tops[j])
+                hit = pb == marks[j]
                 hit_sum = hit_sum + jnp.sum(jnp.where(hit, l, 0.0).reshape(4, 8, 128), axis=0)
-                out_ref[i, 32 * n : 32 * n + 32, 128 * q : 128 * q + 128] = jnp.where(
-                    hit, prob - 1.0, prob
-                ).astype(jnp.bfloat16)
+                out_ref[n, at, 128 * j : 128 * j + 128] = jnp.where(hit, prob - 1.0, prob).astype(jnp.bfloat16)
         acc[...] = hit_sum
 
-    def state_part(b, w_ref, i):
-        out = jnp.dot(w_ref[i], G[...].reshape(Q * B, E), preferred_element_type=jnp.float32)
+    def halves(out):
+        return [[out[256 * u + 64 * i : 256 * u + 64 * i + 64, :] for i in range(4)] for u in (0, 1)]
+
+    def p1_copy(k, h):
+        i = 2 * (k - 1) + h
+        return rcopy(
+            s1.at[k, pl.ds(2 * h, 2)], r1.at[k - 1, pl.ds(2 * h, 2)], g1_s.at[i], g1_r.at[i], near("f", k)
+        )
+
+    def goal_dot(k, h, w_ref, n, u):
+        cols = pl.ds(pl.multiple_of(256 * h, 256), 256)
+        out = jnp.dot(St[256 * u : 256 * u + 256, :], w_ref[n, :, cols], preferred_element_type=jnp.float32)
+        for j in (0, 1):
+            GG[X * wrap(f + k, X) + 2 * h + j, 256 * u : 256 * u + 256, :] = out[:, 128 * j : 128 * j + 128]
+        return [
+            ([out[64 * i : 64 * i + 64, 128 * j : 128 * j + 128] for i in range(4)], s1.at[k, 2 * h + j, u])
+            for j in (0, 1)
+        ]
+
+    def spread_rows(b, carry):
+        at = pl.ds(pl.multiple_of(128 * b, 128), 128)
+        MR[at, :] = jnp.broadcast_to(zr_stat[0, pl.ds(b, 1), :], (128, 128)).T
+        return carry
+
+    lax.fori_loop(0, NB, spread_rows, 0)
+    order = (2, 1, 3, 0)
+    W = (W0, W1)
+
+    def chunk_block(n, mine):
+        pair = lax.rem(z // 2 + H // 2 + jnp.right_shift(156, 2 * n), H)
+        return (c + (1 - mine) * (1 - 2 * c)) * Z + 2 * pair
+
+    def state_term(b, m, out):
+        rows = pl.ds(pl.multiple_of(128 * b, 256), 256)
+        term = jnp.dot(
+            W[m % 2][m // 2, rows, :],
+            G[pl.ds(X * wrap(f + order[m], X), X)].reshape(512, E),
+            preferred_element_type=jnp.float32,
+        )
+        return term if out is None else out + term
+
+    def state_part(n, mine):
+        b = chunk_block(n, mine)
+        out = None
+        for m in range(X):
+            out = state_term(b, m, out)
         GS[pl.ds(b, 2)] = out.reshape(2, 128, E)
 
-    def rb_copy(i, odd):
-        b = chunk_block(i, odd)
+    def rb_copy(n):
+        b = chunk_block(n, 0)
         pair = lax.rem(b, Z) // 2
-        return rcopy(
-            GS.at[pl.ds(b, 2)], GR.at[pl.ds(2 * pair, 2)], rb_s.at[2 * i + odd], rb_r.at[2 * i + odd], sibling
-        )
+        return rcopy(GS.at[pl.ds(b, 2)], GR.at[pl.ds(2 * pair, 2)], rb_s.at[n], rb_r.at[n], sibling)
 
     def rz_copy(s, u, k):
         sg = 0 if s > 0 else 1
@@ -400,59 +436,20 @@
             for i in range(4)
         ]
 
-    def z_step(k):
-        items = [(s, u) for s in signs for u in (0, 1) if k <= (H if u == (s < 0) else H - 1)]
+    def z_step(k, lead):
+        items = [(s, u) for s in signs for u in (0, 1) if lead == (u == (s < 0))]
+        last = k == (H if lead else H - 1)
         ready = []
-        for s, u in items:
-            if k < (H if u == (s < 0) else H - 1):
-                rz_copy(s, u, k + 1).wait_recv()
         for s, u in items:
             at = ((0 if s > 0 else 1) * 2 + u) * H + k
             slabs = gs_slabs(wrap(z + s * k, Z), u)
-            if k < (H if u == (s < 0) else H - 1):
+            if not last:
+                rz_copy(s, u, k + 1).wait_recv()
                 slabs = [a + b for a, b in zip(slabs, restore(zr.at[at]))]
             ready.append((slabs, zs.at[at - 1]))
         quantize_all(ready)
         for s, u in items:
             rz_copy(s, u, k).start()
-
-    weights(chunk_block(0, 0), W0, 0)
-
-    def second_pass(i, carry):
-        b0, b1 = chunk_block(i, 0), chunk_block(i, 1)
-        weights(b1, W1, i)
-        state_part(b0, W0, i)
-        ahead = jnp.minimum(i + 1, 3)
-
-        @pl.when(i < 2)
-        def _():
-            rb_copy(i, 0).start()
-
-        @pl.when(i == 2)
-        def _():
-            rb_copy(0, 0).wait_recv()
-            z_step(H)
-
-        @pl.when(i < 3)
-        def _():
-            weights(chunk_block(ahead, 0), W0, ahead)
-            state_part(b1, W1, i)
-
-        @pl.when(i == 3)
-        def _():
-            state_part(b1, W1, i)
-
-        @pl.when(i < 2)
-        def _():
-            rb_copy(i, 1).start()
-
-        return carry
-
-    lax.fori_loop(0, 4, second_pass, 0)
-    for i, odd in ((0, 1), (1, 0), (1, 1)):
-        rb_copy(i, odd).wait_recv()
-
-    loss_s[0] = loss_s[0] - 2.0 * acc[...]
 
     def loss_copy(stage, axis, k):
         i = 4 * stage + k if stage < 2 else 8 + k
@@ -470,49 +467,67 @@
             total = total + loss_r[i]
         return total
 
+
+    def part_and_give(n, carry):
+        state_part(n, 0)
+        rb_copy(n).start()
+        return carry
+
+    def part_only(n, carry):
+        state_part(n, 1)
+        return carry
+
+    first = [chunk_block(0, mine) for mine in (0, 1)]
+    for m in range(X):
+        weights(wrap(f + order[m], X), first[0], W[m % 2], m // 2)
+    out = None
+    for m in range(X):
+        out = state_term(first[0], m, out)
+        weights(wrap(f + order[m], X), first[1], W[m % 2], m // 2)
+    GS[pl.ds(first[0], 2)] = out.reshape(2, 128, E)
+    rb_copy(0).start()
+    state_part(0, 1)
+
+    def group(n):
+        def half(r, carry):
+            ready = []
+            for i in (1, 2, 3):
+                if n > 0 and i < 3:
+                    ready += goal_dot(order[n - 1], r, W[(n - 1) % 2], (n - 1) // 2, i - 1)
+                weights(wrap(f + order[n], X), chunk_block(i, r), W[n % 2], n // 2)
+            if n > 0:
+                quantize_all(ready)
+                p1_copy(order[n - 1], r).start()
+            return carry
+
+        lax.fori_loop(0, 2, half, 0)
+
+    group(0)
+    rb_copy(0).wait_recv()
+    z_step(H, True)
+    for n in range(1, X):
+        group(n)
+    loss_s[0] = loss_s[0] - 2.0 * acc[...]
     l0 = loss_share(0, "f", X)
-
-    def p1_copy(k, h):
-        i = 2 * (k - 1) + h
-        return rcopy(
-            s1.at[k, pl.ds(2 * h, 2)], r1.at[k - 1, pl.ds(2 * h, 2)], g1_s.at[i], g1_r.at[i], near("f", k)
-        )
-
-    def halves(out):
-        return [[out[256 * u + 64 * i : 256 * u + 64 * i + 64, :] for i in range(4)] for u in (0, 1)]
-
-    def goal_pass(i, carry):
-        k = lax.rem(jnp.right_shift(54, 2 * i), 4)
-        ff = wrap(f + k, X)
-        ready = []
-        for h in (0, 1):
-            at = pl.ds(pl.multiple_of((X * ff + 2 * h) * 128, 256), 256)
-            out = jnp.dot(St0[...], W0[:, :, at].reshape(1024, 256), preferred_element_type=jnp.float32)
-            out = out + jnp.dot(St1[...], W1[:, :, at].reshape(1024, 256), preferred_element_type=jnp.float32)
-            for j in (0, 1):
-                block = out[:, 128 * j : 128 * j + 128]
-                GG[X * ff + 2 * h + j] = block
-                for u, slabs in enumerate(halves(block)):
-                    ready.append((slabs, s1.at[k, 2 * h + j, u]))
-            quantize_all(ready[4 * h :])
-
-            @pl.when(i < 3)
-            def _():
-                p1_copy(k, h).start()
-
-        @pl.when(i == 0)
-        def _():
-            z_step(H - 1)
-
-        @pl.when(i == 3)
-        def _():
-            z_step(H - 2)
-
-        return carry
-
-    lax.fori_loop(0, X, goal_pass, 0)
+    lax.fori_loop(1, 4, part_and_give, 0)
+    lax.fori_loop(1, 4, part_only, 0)
+    for n in range(1, 4):
+        rb_copy(n).wait_recv()
+    z_step(H - 1, False)
+    z_step(H - 1, True)
+
+    def own_goal(h, carry):
+        for u in (0, 1):
+            goal_dot(0, h, W[1], 1, u)
+        return carry
+
+    lax.fori_loop(0, 2, own_goal, 0)
     loss_s[1] = loss_add(0, l0, range(1, X))
     l1 = loss_share(1, "g", X)
+    z_step(H - 2, False)
+    z_step(H - 2, True)
+    loss_s[2] = loss_add(1, l1, range(5, 4 + X))
+    l2 = loss_share(2, "z", Z)
 
     def p2_copy(k):
         return rcopy(s2.at[k - 1], r2.at[k - 1], g2_s.at[k - 1], g2_r.at[k - 1], near("g", k))
@@ -524,18 +539,25 @@
                 blocks[u] = [a + b for a, b in zip(blocks[u], restore(r1.at[k - 1, gg, u]))]
         return blocks
 
-    for k in (2, 1):
+    for k in (2, 1, 3):
         for h in (0, 1):
             p1_copy(k, h).wait_recv()
-    loss_s[2] = loss_add(1, l1, range(5, 4 + X))
-    l2 = loss_share(2, "z", Z)
-    z_step(1)
-    for h in (0, 1):
-        p1_copy(3, h).wait_recv()
     for k in (2, 1, 3):
         quantize_all([(slabs, s2.at[k - 1, u]) for u, slabs in enumerate(summed(wrap(g + k, X)))])
         p2_copy(k).start()
+    z_step(1, False)
+    z_step(1, True)
     mine = summed(g)
+    for k in (1, 3, 2):
+        p2_copy(k).wait_recv()
+        for u in (0, 1):
+            mine[u] = [a + b for a, b in zip(mine[u], restore(r2.at[k - 1, u]))]
+    for u in (0, 1):
+        for i, part in enumerate(mine[u]):
+            GG[home, 256 * u + 64 * i : 256 * u + 64 * i + 64, :] = part
+    out_goal[...] = GG[home].T
+    gg_store = pltpu.make_async_copy(out_goal, gg_out, in_sem.at[1])
+    gg_store.start()
     loss_s[3] = loss_add(2, l2, range(9, 8 + Z))
 
     def loss_last():
@@ -551,24 +573,13 @@
             GS[c * Z + z, 64 * u : 64 * u + 64, 128 * i : 128 * i + 128] = part
     gs_store = pltpu.make_async_copy(GS.at[c * Z + z], gs_out, in_sem.at[0])
     gs_store.start()
-    for k in (1, 3, 2):
-        p2_copy(k).wait_recv()
-        for u in (0, 1):
-            mine[u] = [a + b for a, b in zip(mine[u], restore(r2.at[k - 1, u]))]
-    for u in (0, 1):
-        for i, part in enumerate(mine[u]):
-            GG[home, 256 * u + 64 * i : 256 * u + 64 * i + 64, :] = part
-    out_goal[...] = GG[home].T
-    gg_store = pltpu.make_async_copy(out_goal, gg_out, in_sem.at[1])
-    gg_store.start()
     total = loss_add(3, [loss_last()], [0])
     loss_out[0, 0] = jnp.sum(total) * (LN2 / (4.0 * Q * Z * B))
 
     for make, args in started:
         make(*args).wait_send()
-    for i in (0, 1):
-        for odd in (0, 1):
-            rb_copy(i, odd).wait_send()
+    for n in range(4):
+        rb_copy(n).wait_send()
     for k in range(1, X):
         for h in (0, 1):
             p1_copy(k, h).wait_send()
@@ -597,8 +608,7 @@
     dma = pltpu.SemaphoreType.DMA
     scratch = [
         vmem((2, Z, B, E), bf16), vmem((Q, B, E), bf16), vmem((2, Z, B), jnp.int32),
-        vmem((R, C), f32), vmem((4, 256, C), bf16), vmem((4, 256, C), bf16),
-        vmem((E, R // 2), bf16), vmem((E, R // 2), bf16),
+        vmem((R, C), f32), vmem((2, R, C // 4), bf16), vmem((2, R, C // 4), bf16), vmem((E, R), bf16),
         vmem((NB, B, E), f32), vmem((Z, B, E), f32), vmem((Q, E, B), f32),
         vmem((R, B), f32), vmem((R, B), f32), vmem((R, B), f32), vmem((8, C), f32), vmem((8, C), f32),
         vmem((NB, B), f32), vmem((Z, NB, B), f32), vmem((NB, B), f32), vmem((NB, B), f32),

time: 85.6 us -> 82.3 us (0.961)
  Pallas kernels: 84.8 us -> 81.5 us
    pallas_call x1, Pallas kernels: 82.3 us -> 79 us  [body(): pl.pallas_call(functools.partial(kernel, Z), out_shape=shapes, in_specs=[...]
where the time goes in v3:
time: 82.3 us; the launch traced here: 82.2 us
  Pallas kernels  81.5 us (99%)
    pallas_call x1, Pallas kernels, body(): pl.pallas_call(functools.partial(kernel, Z), out_shape=shapes, in_specs=[...  79 us
    pallas_call x1, Pallas kernels, body(): pl.pallas_call(hand_over, out_shape=shapes, in_specs=[whole, whole, scala...  2.48 us

profile of v3, /device:TPU:1, one launch (start us, length us, event | category | flops | bytes accessed | tf_op | source)
XLA Modules:
  0.0 82.2 jit_solution(6413902010196337440)
XLA Ops:
  0.6 79.0 %shard_map.58 = (f32[128,512]{1,0:T(8,128)}, f32[128,512]{1,0:T(8,128)}, f32[1,1]{1,0:T(1,128)}) custom-call(bf16[128,512]{1,0:T(8,128)(2,1)} %state_ref.1, bf16[128,512]{1,0:T(8,128)(2,1)} %goal_ref.1, s32[8,128]{1,0:T(8,128)} %bitcast.2), custom_call_target="tpu_custom_call" | custom-call | tf_op jit(solution)/shard_map/pallas_call | solution.py:633
  79.7 2.5 %shard_map.59 = (f32[128,512]{1,0:T(8,128)}, f32[128,512]{1,0:T(8,128)}, f32[1,1]{1,0:T(1,128)}) custom-call(f32[128,512]{1,0:T(8,128)} %get-tuple-element.9.gs_in, f32[128,512]{1,0:T(8,128)} %get-tuple-element.10.gg_in, f32[1,1]{1,0:T(1,128)} %get-tuple-element.11.loss_in), custom_call_target="tpu_custom_call" | custom-call | tf_op jit(solution)/shard_map/pallas_call | solution.py:643

commit v4 on v3

--- a/solution.py
+++ b/solution.py
@@ -451,22 +451,23 @@
         for s, u in items:
             rz_copy(s, u, k).start()
 
-    def loss_copy(stage, axis, k):
-        i = 4 * stage + k if stage < 2 else 8 + k
-        return rcopy(loss_s.at[stage], loss_r.at[i], st_s.at[32 + i], st_r.at[32 + i], near(axis, k))
-
-    def loss_share(stage, axis, n):
-        for k in range(1, n):
-            start(loss_copy, stage, axis, k)
-        return [loss_copy(stage, axis, k) for k in range(1, n)]
-
-    def loss_add(stage, copies, slots):
-        arrive(copies)
+    def loss_copy(stage, k):
+        i = (0, 0, 4, 8)[stage] + k
+        to = sibling if stage == 0 else near(" fgz"[stage], k)
+        return rcopy(loss_s.at[stage], loss_r.at[i], st_s.at[32 + i], st_r.at[32 + i], to)
+
+    loss_peers = ((0,), range(1, X), range(1, X), range(1, Z))
+
+    def loss_share(stage):
+        for k in loss_peers[stage]:
+            start(loss_copy, stage, k)
+
+    def loss_add(stage):
         total = loss_s[stage]
-        for i in slots:
-            total = total + loss_r[i]
+        for k in loss_peers[stage]:
+            loss_copy(stage, k).wait_recv()
+            total = total + loss_r[(0, 0, 4, 8)[stage] + k]
         return total
-
 
     def part_and_give(n, carry):
         state_part(n, 0)
@@ -490,44 +491,48 @@
 
     def group(n):
         def half(r, carry):
-            ready = []
             for i in (1, 2, 3):
-                if n > 0 and i < 3:
-                    ready += goal_dot(order[n - 1], r, W[(n - 1) % 2], (n - 1) // 2, i - 1)
                 weights(wrap(f + order[n], X), chunk_block(i, r), W[n % 2], n // 2)
-            if n > 0:
+            return carry
+
+        lax.fori_loop(0, 2, half, 0)
+
+    def goals(n):
+        def half(h, carry):
+            ready = goal_dot(order[n], h, W[n % 2], n // 2, 0)
+            ready += goal_dot(order[n], h, W[n % 2], n // 2, 1)
+            if order[n] > 0:
                 quantize_all(ready)
-                p1_copy(order[n - 1], r).start()
+                p1_copy(order[n], h).start()
             return carry
 
         lax.fori_loop(0, 2, half, 0)
 
-    group(0)
-    rb_copy(0).wait_recv()
-    z_step(H, True)
-    for n in range(1, X):
+    for n in range(X):
         group(n)
+        if n < X - 1:
+            goals(n)
+        if n == 0:
+            rb_copy(0).wait_recv()
+            z_step(H, True)
     loss_s[0] = loss_s[0] - 2.0 * acc[...]
-    l0 = loss_share(0, "f", X)
-    lax.fori_loop(1, 4, part_and_give, 0)
-    lax.fori_loop(1, 4, part_only, 0)
-    for n in range(1, 4):
+    loss_share(0)
+    lax.fori_loop(1, 3, part_and_give, 0)
+    loss_s[1] = loss_add(0)
+    loss_share(1)
+    lax.fori_loop(1, 3, part_only, 0)
+    for n in (1, 2):
         rb_copy(n).wait_recv()
+    z_step(H - 1, True)
     z_step(H - 1, False)
-    z_step(H - 1, True)
-
-    def own_goal(h, carry):
-        for u in (0, 1):
-            goal_dot(0, h, W[1], 1, u)
-        return carry
-
-    lax.fori_loop(0, 2, own_goal, 0)
-    loss_s[1] = loss_add(0, l0, range(1, X))
-    l1 = loss_share(1, "g", X)
+    lax.fori_loop(3, 4, part_and_give, 0)
+    lax.fori_loop(3, 4, part_only, 0)
+    goals(X - 1)
+    rb_copy(3).wait_recv()
+    loss_s[2] = loss_add(1)
+    loss_share(2)
+    z_step(H - 2, True)
     z_step(H - 2, False)
-    z_step(H - 2, True)
-    loss_s[2] = loss_add(1, l1, range(5, 4 + X))
-    l2 = loss_share(2, "z", Z)
 
     def p2_copy(k):
         return rcopy(s2.at[k - 1], r2.at[k - 1], g2_s.at[k - 1], g2_r.at[k - 1], near("g", k))
@@ -545,8 +550,10 @@
     for k in (2, 1, 3):
         quantize_all([(slabs, s2.at[k - 1, u]) for u, slabs in enumerate(summed(wrap(g + k, X)))])
         p2_copy(k).start()
+    loss_s[3] = loss_add(2)
+    loss_share(3)
+    z_step(1, True)
     z_step(1, False)
-    z_step(1, True)
     mine = summed(g)
     for k in (1, 3, 2):
         p2_copy(k).wait_recv()
@@ -558,12 +565,6 @@
     out_goal[...] = GG[home].T
     gg_store = pltpu.make_async_copy(out_goal, gg_out, in_sem.at[1])
     gg_store.start()
-    loss_s[3] = loss_add(2, l2, range(9, 8 + Z))
-
-    def loss_last():
-        return rcopy(loss_s.at[3], loss_r.at[0], st_s.at[32], st_r.at[32], sibling)
-
-    start(loss_last)
     for u in (0, 1):
         slabs = gs_slabs(z, u)
         for s in signs:
@@ -573,7 +574,7 @@
             GS[c * Z + z, 64 * u : 64 * u + 64, 128 * i : 128 * i + 128] = part
     gs_store = pltpu.make_async_copy(GS.at[c * Z + z], gs_out, in_sem.at[0])
     gs_store.start()
-    total = loss_add(3, [loss_last()], [0])
+    total = loss_add(3)
     loss_out[0, 0] = jnp.sum(total) * (LN2 / (4.0 * Q * Z * B))
 
     for make, args in started:

time: 82.3 us -> 79.9 us (0.971)
  Pallas kernels: 81.5 us -> 79.1 us
    pallas_call x1, Pallas kernels: 79 us -> 76.6 us  [body(): pl.pallas_call(functools.partial(kernel, Z), out_shape=shapes, in_specs=[...]
where the time goes in v4:
time: 79.9 us; the launch traced here: 79.7 us
  Pallas kernels  79.1 us (99%)
    pallas_call x1, Pallas kernels, body(): pl.pallas_call(functools.partial(kernel, Z), out_shape=shapes, in_specs=[...  76.6 us
    pallas_call x1, Pallas kernels, body(): pl.pallas_call(hand_over, out_shape=shapes, in_specs=[whole, whole, scala...  2.48 us

profile of v4, /device:TPU:1, one launch (start us, length us, event | category | flops | bytes accessed | tf_op | source)
XLA Modules:
  0.0 79.7 jit_solution(14478825095018480)
XLA Ops:
  0.6 76.6 %shard_map.58 = (f32[128,512]{1,0:T(8,128)}, f32[128,512]{1,0:T(8,128)}, f32[1,1]{1,0:T(1,128)}) custom-call(bf16[128,512]{1,0:T(8,128)(2,1)} %state_ref.1, bf16[128,512]{1,0:T(8,128)(2,1)} %goal_ref.1, s32[8,128]{1,0:T(8,128)} %bitcast.2), custom_call_target="tpu_custom_call" | custom-call | tf_op jit(solution)/shard_map/pallas_call | solution.py:634
  77.3 2.5 %shard_map.59 = (f32[128,512]{1,0:T(8,128)}, f32[128,512]{1,0:T(8,128)}, f32[1,1]{1,0:T(1,128)}) custom-call(f32[128,512]{1,0:T(8,128)} %get-tuple-element.9.gs_in, f32[128,512]{1,0:T(8,128)} %get-tuple-element.10.gg_in, f32[1,1]{1,0:T(1,128)} %get-tuple-element.11.loss_in), custom_call_target="tpu_custom_call" | custom-call | tf_op jit(solution)/shard_map/pallas_call | solution.py:644

commit v5 on v4

--- a/solution.py
+++ b/solution.py
@@ -555,6 +555,19 @@
     z_step(1, True)
     z_step(1, False)
     mine = summed(g)
+
+    for make, args in started:
+        make(*args).wait_send()
+    for n in range(4):
+        rb_copy(n).wait_send()
+    for k in range(1, X):
+        for h in (0, 1):
+            p1_copy(k, h).wait_send()
+    for s in signs:
+        for u in (0, 1):
+            for k in range(2, (H if u == (s < 0) else H - 1) + 1):
+                rz_copy(s, u, k).wait_send()
+
     for k in (1, 3, 2):
         p2_copy(k).wait_recv()
         for u in (0, 1):
@@ -577,18 +590,11 @@
     total = loss_add(3)
     loss_out[0, 0] = jnp.sum(total) * (LN2 / (4.0 * Q * Z * B))
 
-    for make, args in started:
-        make(*args).wait_send()
-    for n in range(4):
-        rb_copy(n).wait_send()
     for k in range(1, X):
-        for h in (0, 1):
-            p1_copy(k, h).wait_send()
         p2_copy(k).wait_send()
     for s in signs:
         for u in (0, 1):
-            for k in range(1, (H if u == (s < 0) else H - 1) + 1):
-                rz_copy(s, u, k).wait_send()
+            rz_copy(s, u, 1).wait_send()
     gs_store.wait()
     gg_store.wait()
 

time: 79.9 us -> 79.9 us (level)
  no operation moved by 1% of the time
where the time goes in v5:
time: 79.9 us; the launch traced here: 79.7 us
  Pallas kernels  79.1 us (99%)
    pallas_call x1, Pallas kernels, body(): pl.pallas_call(functools.partial(kernel, Z), out_shape=shapes, in_specs=[...  76.6 us
    pallas_call x1, Pallas kernels, body(): pl.pallas_call(hand_over, out_shape=shapes, in_specs=[whole, whole, scala...  2.48 us

profile of v5, /device:TPU:1, one launch (start us, length us, event | category | flops | bytes accessed | tf_op | source)
XLA Modules:
  0.0 79.7 jit_solution(15702948562619070081)
XLA Ops:
  0.6 76.6 %shard_map.58 = (f32[128,512]{1,0:T(8,128)}, f32[128,512]{1,0:T(8,128)}, f32[1,1]{1,0:T(1,128)}) custom-call(bf16[128,512]{1,0:T(8,128)(2,1)} %state_ref.1, bf16[128,512]{1,0:T(8,128)(2,1)} %goal_ref.1, s32[8,128]{1,0:T(8,128)} %bitcast.2), custom_call_target="tpu_custom_call" | custom-call | tf_op jit(solution)/shard_map/pallas_call | solution.py:640
  77.3 2.5 %shard_map.59 = (f32[128,512]{1,0:T(8,128)}, f32[128,512]{1,0:T(8,128)}, f32[1,1]{1,0:T(1,128)}) custom-call(f32[128,512]{1,0:T(8,128)} %get-tuple-element.9.gs_in, f32[128,512]{1,0:T(8,128)} %get-tuple-element.10.gg_in, f32[1,1]{1,0:T(1,128)} %get-tuple-element.11.loss_in), custom_call_target="tpu_custom_call" | custom-call | tf_op jit(solution)/shard_map/pallas_call | solution.py:650
